TPU v7x, 32 devices: a whole 2x2x4 slice. The times are simulated.
32 devices in a mesh: groups: 2 (over x), seq: 8 (over z, y), head: 2 (over core).
Axes of the slice: x: 2, y: 2, z: 4, core: 2. Of those that a mesh axis runs over, the one named last changes fastest.
Arguments:
- queries: bfloat16 [16384, 1536], P(('groups', 'seq', 'head')), parts along dimension 0, may hold values from -5 to 5
- keys: bfloat16 [16384, 1536], P(('groups', 'seq', 'head')), parts along dimension 0, may hold values from -5 to 5
- values: bfloat16 [16384, 1536], P(('groups', 'seq', 'head')), parts along dimension 0, may hold values from -6 to 6
- tile_lists: int32 [256, 24], P('groups'), parts along dimension 0, may hold values from 0 to 127, as said below
Outputs:
- attended: bfloat16 [16384, 1536], P(('groups', 'seq', 'head')), parts along dimension 0
There are 2 independent parts, one for each index of `groups`. A program takes and returns all parts, laid end to end along the dimension named above; each array names one. Nothing has to cross between parts.
Inputs may be any that keep to these rules, and one draw needn't show every extreme that they name: `tile_lists`: each row names 24 distinct tiles. Cut the tiles into runs of 16 consecutive ones: the rows of one run together name at most 8 distinct tiles of any run, exactly 8 tiles of half of the runs and 4 of the others.
All inputs are finite; a program needn't handle non-finite values.
Results may differ from a plain program's by a relative error of at most 0.0042.
Values may be sent and summed in bfloat16 or wider, within the bound.
No kernel may reach another device: no remote copies, remote signals or barrier semaphores. Data moves between devices by JAX's collectives and lax.ppermute only.
A program may use at most 128 MiB of HBM per device.

v0:
```python
import jax
import jax.numpy as jnp
from jax import lax
from jax.sharding import PartitionSpec as P

HD = 128
TILE = 64


def score_tile(key_flat, score_scale, query_tile, row_index):
    gathered = key_flat[row_index]
    scores = (
        jnp.einsum("qhd,khtd->hqkt", query_tile, gathered, preferred_element_type=jnp.float32)
        * score_scale
    )
    row_top = jnp.max(scores, axis=(2, 3), keepdims=True)
    weights = jnp.exp(scores - row_top)
    row_total = jnp.sum(weights, axis=(2, 3))
    return (weights.astype(jnp.bfloat16), row_total)


def mix_tile(value_flat, rounded, row_total, row_index):
    gathered = value_flat[row_index]
    mixture = jnp.einsum("hqkt,khtd->qhd", rounded, gathered, preferred_element_type=jnp.float32)
    mixture = mixture / jnp.transpose(row_total)[:, :, None]
    return mixture.astype(jnp.bfloat16).reshape(mixture.shape[0], -1)


def select_slots(
    pick_table, arrays, seq_count, capacity, shard_tiles, tile_rows, local_heads, head_dim
):
    count = len(arrays)
    stacked = jnp.stack(arrays, 0).reshape(count, shard_tiles, tile_rows, local_heads, head_dim)
    stacked = stacked.transpose(1, 0, 3, 2, 4).reshape(shard_tiles, -1)
    outgoing = jnp.dot(pick_table, stacked, preferred_element_type=jnp.float32).astype(jnp.bfloat16)
    return outgoing.reshape(seq_count, capacity, count, local_heads, tile_rows, head_dim)


def per_device(queries, keys, values, tile_lists):
    seq_count = lax.axis_size("seq")
    head_count = lax.axis_size("head")
    head_dim = HD
    tile_rows = TILE
    total_tiles, top_count = tile_lists.shape
    local_heads = queries.shape[1] // head_dim // head_count
    local_rows = queries.shape[0] * head_count
    shard_tiles = local_rows // tile_rows
    capacity = 64 // seq_count
    seq_index = lax.axis_index("seq")
    score_scale = head_dim ** (-0.5)
    tile_ids = seq_index * shard_tiles + jnp.arange(shard_tiles, dtype=jnp.int32)
    by_run = tile_lists.reshape(seq_count, shard_tiles * top_count)
    need_out = jnp.any(by_run[:, :, None] == tile_ids[None, None, :], axis=1)
    slot_out = jnp.cumsum(need_out.astype(jnp.int32), axis=1) - 1
    slot_ids = jnp.arange(capacity, dtype=jnp.int32)
    pick_table = need_out[:, None, :] & (slot_out[:, None, :] == slot_ids[None, :, None])
    pick_table = pick_table.astype(jnp.bfloat16).reshape(seq_count * capacity, shard_tiles)
    own_lists = lax.dynamic_slice_in_dim(tile_lists, seq_index * shard_tiles, shard_tiles, 0)
    all_ids = jnp.arange(total_tiles, dtype=jnp.int32)
    matches = own_lists[:, :, None] == all_ids[None, None, :]
    listed = jnp.any(matches, axis=1).reshape(shard_tiles, seq_count, shard_tiles)
    need_in = jnp.any(listed, axis=0)
    slot_in = jnp.cumsum(need_in.astype(jnp.int32), axis=1) - 1
    queries_local, keys_local, values_local = (
        lax.all_to_all(queries, "head", split_axis=1, concat_axis=0, tiled=True),
        lax.all_to_all(keys, "head", split_axis=1, concat_axis=0, tiled=True),
        lax.all_to_all(values, "head", split_axis=1, concat_axis=0, tiled=True),
    )
    received = lax.all_to_all(
        select_slots(
            pick_table,
            (keys_local, values_local),
            seq_count,
            capacity,
            shard_tiles,
            tile_rows,
            local_heads,
            head_dim,
        ),
        "seq",
        split_axis=0,
        concat_axis=0,
        tiled=True,
    )
    key_slots = received[:, :, 0]
    value_slots = received[:, :, 1]
    flat_slots = jnp.broadcast_to(slot_in.reshape(1, 1, total_tiles), matches.shape)
    listed_slot = jnp.sum(jnp.where(matches, flat_slots, 0), axis=2)
    source_run = own_lists // shard_tiles
    slot_index = source_run * capacity + listed_slot
    query_tiles = queries_local.reshape(shard_tiles, tile_rows, local_heads, head_dim)
    slot_shape = (seq_count * capacity, local_heads, tile_rows, head_dim)
    key_flat = key_slots.reshape(slot_shape)
    value_flat = value_slots.reshape(slot_shape)

    def joined_tile(args):
        rounded, row_total = score_tile(key_flat, score_scale, args[0], args[1])
        return mix_tile(value_flat, rounded, row_total, args[1])

    attended = lax.map(joined_tile, (query_tiles, slot_index))
    attended = attended.reshape(local_rows, local_heads * head_dim)
    return lax.all_to_all(attended, "head", split_axis=0, concat_axis=1, tiled=True)


def solution(mesh):
    placed = (
        P(("groups", "seq", "head"), None),
        P(("groups", "seq", "head"), None),
        P(("groups", "seq", "head"), None),
        P("groups", None),
    )
    return jax.shard_map(
        per_device,
        mesh=mesh,
        in_specs=placed,
        out_specs=P(("groups", "seq", "head"), None),
        check_vma=False,
    )
```

profile of v0, /device:TPU:18, one launch (start us, length us, event | category | flops | bytes accessed | tf_op | source)
XLA Modules:
  0.0 585.8 jit_solution(16037402812458152717)
XLA Ops:
  2.7 3.8 all-to-all-start.1
  8.9 4.6 all-to-all-start
  19.7 4.7 all-to-all-start.3
  24.3 4.3 stack.9
  32.1 11.0 %convolution_convert_fusion = bf16[64,98304]{1,0:T(8,128)(2,1)} fusion(bf16[2,8,768,128]{3,2,1,0:T(8,128)(2,1)S(1)} %bitcast.73, s32[8,16]{1,0:T(8,128)S(1)} %broadcast_add_fusion, pred[8,16]{1,0:T(8,128)(4,1)S(1)} %compare_reduce_fusion), kind=kOutput, calls=%fused_computation.22 | convolution fusion | flops 207620096 | bytes 15729280 | tf_op jit(solution)/shard_map/dot_general | solution.py:35
  43.0 6.2 %all-to-all-start.2 = ((bf16[8,8,2,6,64,128]{5,1,4,3,2,0:T(8,128)(2,1)}), bf16[8,8,2,6,64,128]{5,1,4,3,2,0:T(8,128)(2,1)}, u32[]{:S(2)}, u32[]{:S(2)}) async-start(bf16[8,8,2,6,64,128]{5,1,4,3,2,0:T(8,128)(2,1)} %bitcast.72), calls=%async_computation.2 | async-start | bytes 25165824 | tf_op jit(solution)/shard_map/all_to_all | solution.py:69
  55.2 264.3 %all-to-all-done.2 = bf16[8,8,2,6,64,128]{5,1,4,3,2,0:T(8,128)(2,1)} async-done(((bf16[8,8,2,6,64,128]{5,1,4,3,2,0:T(8,128)(2,1)}), bf16[8,8,2,6,64,128]{5,1,4,3,2,0:T(8,128)(2,1)}, u32[]{:S(2)}, u32[]{:S(2)}) %all-to-all-start.2) | async-done | bytes 12582944 | tf_op jit(solution)/shard_map/all_to_all | solution.py:69
  319.5 5.4 fusion.32
  324.9 4.4 copy.60
  329.4 4.4 copy.62
  333.8 243.6 %while.10 = (s32[]{:T(128)}, bf16[16,64,768]{2,1,0:T(8,128)(2,1)}, s32[16,24]{1,0:T(8,128)S(1)}, bf16[64,6,64,128]{3,2,1,0:T(8,128)(2,1)}, bf16[16,64,6,128]{3,1...) while((s32[]{:T(128)}, bf16[16,64,768]{2,1,0:T(8,128)(2,1)}, s32[16,24]{1,0:T(8,128)S(1)}, ...), condition=%wide.region_8.9_spmd, body=%wide.region_5.8_spmd.sunk | while | flops 305627456 | bytes 22031920 | solution.py:100
  333.8 3.8 gather_fusion.1
  349.1 3.8 gather_fusion.1
  364.3 3.8 gather_fusion.1
  372.3 3.8 gather_fusion
  379.5 3.8 gather_fusion.1
  387.5 3.8 gather_fusion
  394.7 3.8 gather_fusion.1
  410.0 3.8 gather_fusion.1
  425.2 3.8 gather_fusion.1
  440.4 3.8 gather_fusion.1
  455.6 3.8 gather_fusion.1
  470.9 3.8 gather_fusion.1
  478.9 3.8 gather_fusion
  486.1 3.8 gather_fusion.1
  501.3 3.8 gather_fusion.1
  516.5 3.8 gather_fusion.1
  531.8 3.8 gather_fusion.1
  547.0 3.8 gather_fusion.1
  562.2 3.8 gather_fusion.1
  570.2 3.8 gather_fusion
  577.4 6.1 %all_to_all.72 = bf16[2,512,768]{2,1,0:T(8,128)(2,1)S(1)} all-to-all(bf16[2,512,768]{2,1,0:T(8,128)(2,1)} %bitcast.80), channel_id=1, replica_groups=mesh['groups'=2,'seq'=8,'head'=2] {'head'}, dimensions={0} | all-to-all | bytes 3145728 | tf_op jit(solution)/shard_map/all_to_all | solution.py:102
  (176 shorter events, 190.2 us)
Async XLA Ops:
  2.7 3.8 copy-start.2
  2.7 4.5 copy-start.1
  2.7 6.3 %all-to-all-start.1 = ((bf16[512,2,768]{2,0,1:T(8,128)(2,1)}), bf16[512,2,768]{2,0,1:T(8,128)(2,1)S(1)}, u32[]{:S(2)}, u32[]{:S(2)}) async-start(bf16[512,2,768]{2,0,1:T(8,128)(2,1)} %bitcast.56), calls=%async_computation.1 | async-start | bytes 3145728 | tf_op jit(solution)/shard_map/all_to_all | solution.py:67
  8.9 4.6 copy-start
  8.9 10.7 %all-to-all-start = ((bf16[512,2,768]{2,0,1:T(8,128)(2,1)}), bf16[512,2,768]{2,0,1:T(8,128)(2,1)}, u32[]{:S(2)}, u32[]{:S(2)}) async-start(bf16[512,2,768]{2,0,1:T(8,128)(2,1)} %bitcast.57), calls=%async_computation | async-start | bytes 3145728 | tf_op jit(solution)/shard_map/all_to_all | solution.py:66
  19.7 23.4 %all-to-all-start.3 = ((bf16[512,2,768]{2,0,1:T(8,128)(2,1)}), bf16[512,2,768]{2,0,1:T(8,128)(2,1)}, u32[]{:S(2)}, u32[]{:S(2)}) async-start(bf16[512,2,768]{2,0,1:T(8,128)(2,1)} %bitcast.75), calls=%async_computation.3 | async-start | bytes 3145728 | tf_op jit(solution)/shard_map/all_to_all | solution.py:65
  43.0 276.5 %all-to-all-start.2 = ((bf16[8,8,2,6,64,128]{5,1,4,3,2,0:T(8,128)(2,1)}), bf16[8,8,2,6,64,128]{5,1,4,3,2,0:T(8,128)(2,1)}, u32[]{:S(2)}, u32[]{:S(2)}) async-start(bf16[8,8,2,6,64,128]{5,1,4,3,2,0:T(8,128)(2,1)} %bitcast.72), calls=%async_computation.2 | async-start | bytes 25165824 | tf_op jit(solution)/shard_map/all_to_all | solution.py:69
where the time goes:
time: 593 us; the launch traced here: 586 us
  waiting for transfers between devices  265 us (45%)
  local copies, waits for them, and re-layouts  172 us (29%)
  matrix products  78.2 us (13%)
  other arithmetic  44.7 us (8%)
  starting transfers between devices  19.3 us (3%)
  blocking collectives  6.15 us (1%)
    all_to_all x1, waiting for transfers between devices, per_device(): lax.all_to_all(select_slots(pick_table, (keys_local, values_local), seq_c...  264 us
    gather x16, local copies, waits for them, and re-layouts, score_tile(): gathered = key_flat[row_index]  60.5 us
    gather x16, local copies, waits for them, and re-layouts, mix_tile(): gathered = value_flat[row_index]  60.5 us
    reduce_sum x16, other arithmetic, score_tile(): row_total = jnp.sum(weights, axis=(2, 3))  40.7 us
    dot_general x16, matrix products, mix_tile(): jnp.einsum('hqkt,khtd->qhd', rounded, gathered, preferred_element_type=jn...  40.6 us
    dot_general x16, matrix products, score_tile(): jnp.einsum('qhd,khtd->hqkt', query_tile, gathered, preferred_element_type...  26.6 us
  transfers between devices with their start and end apart: 4, of which 2 were waited for; matrix products, arithmetic and copies ran while one was open for 6% of the time, Pallas kernels for 0%

commit v1 on v0

--- a/solution.py
+++ b/solution.py
@@ -1,7 +1,12 @@
+import functools
+import math
+
 import jax
 import jax.numpy as jnp
 from jax import lax
-from jax.sharding import PartitionSpec as P
+from jax.experimental import pallas as pl
+from jax.experimental.pallas import tpu as pltpu
+from jax.sharding import Mesh, PartitionSpec as P
 
 HD = 128
 TILE = 64
@@ -36,7 +41,7 @@
     return outgoing.reshape(seq_count, capacity, count, local_heads, tile_rows, head_dim)
 
 
-def per_device(queries, keys, values, tile_lists):
+def slot_plan(queries, keys, values, tile_lists):
     seq_count = lax.axis_size("seq")
     head_count = lax.axis_size("head")
     head_dim = HD
@@ -102,17 +107,181 @@
     return lax.all_to_all(attended, "head", split_axis=0, concat_axis=1, tiled=True)
 
 
+PLANES = 4
+SIDE = 2
+AXES = ("groups", "z", "y", "head")
+SWAP = [(0, 1), (1, 0), (2, 3), (3, 2)]
+INWARD = [(0, 1), (3, 2)]
+OUTWARD = [(1, 0), (2, 3)]
+CROSS = [(1, 2), (2, 1)]
+EXPONENT = HD**-0.5 * math.log2(math.e)
+UNROLL = 4
+
+
+def attend_kernel(count, lists, *refs, top_count, sources, slots):
+    ends, queries = refs[0], refs[1 : 1 + sources]
+    picks = refs[1 + sources : 1 + sources + 2 * slots]
+    out, query_buf, key_buf, value_buf, sems = refs[1 + sources + 2 * slots :]
+    tiles = key_buf.shape[0] // PLANES
+    own = queries[0].shape[0]
+    at_end = ends[0] == 1
+
+    def move(src, dst, sem):
+        return pltpu.make_async_copy(src, dst, sem)
+
+    def part(buf, slot):
+        return buf.at[pl.ds(slot * tiles, tiles)]
+
+    @pl.when(count[0] > 0)
+    def _():
+        for at, ref in enumerate(queries):
+            move(ref, query_buf.at[pl.ds(at * own, own)], sems.at[0]).start()
+        for kind, buf in enumerate((key_buf, value_buf)):
+            given = picks[kind * slots : (kind + 1) * slots]
+            for slot in range(2):
+                move(given[slot], part(buf, slot), sems.at[1 + kind]).start()
+            if slots == PLANES:
+                for slot in range(2, PLANES):
+                    move(given[slot], part(buf, slot), sems.at[1 + kind]).start()
+            else:
+
+                @pl.when(at_end)
+                def _():
+                    for slot in range(2, PLANES):
+                        move(given[slot + 2], part(buf, slot), sems.at[1 + kind]).start()
+
+                @pl.when(jnp.logical_not(at_end))
+                def _():
+                    for slot in range(2, PLANES):
+                        move(given[slot], part(buf, slot), sems.at[1 + kind]).start()
+
+        move(query_buf, query_buf, sems.at[0]).wait()
+        move(key_buf, key_buf, sems.at[1]).wait()
+        move(value_buf, value_buf, sems.at[2]).wait()
+
+    def one(row):
+        keys = jnp.concatenate([key_buf[lists[row, t]] for t in range(top_count)], axis=0)
+        scores = lax.dot_general(
+            query_buf[row], keys, (((1,), (1,)), ((), ())), preferred_element_type=jnp.float32
+        )
+        row_top = jnp.max(scores, axis=1, keepdims=True)
+        weights = jnp.exp2((scores - row_top) * EXPONENT)
+        row_total = jnp.sum(weights, axis=1, keepdims=True)
+        values = jnp.concatenate([value_buf[lists[row, t]] for t in range(top_count)], axis=0)
+        mixture = jnp.dot(weights.astype(jnp.bfloat16), values, preferred_element_type=jnp.float32)
+        out[row] = (mixture / row_total).astype(jnp.bfloat16)
+
+    def step(at, carry):
+        for sub in range(UNROLL):
+            one(at * UNROLL + sub)
+        return carry
+
+    lax.fori_loop(0, count[0] // UNROLL, step, 0)
+
+
+def attend(count, lists, ends, queries, keys, values):
+    sources, slots = len(queries), len(keys)
+    tiles = queries[0].shape[0]
+    top_count = lists.shape[1]
+    rows = sources * tiles
+    kernel = functools.partial(attend_kernel, top_count=top_count, sources=sources, slots=slots)
+    work = 4 * rows * TILE * top_count * TILE * HD
+    return pl.pallas_call(
+        kernel,
+        out_shape=jax.ShapeDtypeStruct((rows, TILE, HD), jnp.bfloat16),
+        in_specs=[pl.BlockSpec(memory_space=pltpu.SMEM)] * 3
+        + [pl.BlockSpec(memory_space=pl.ANY)] * (sources + 2 * slots),
+        out_specs=pl.BlockSpec(memory_space=pltpu.VMEM),
+        scratch_shapes=[
+            pltpu.VMEM((rows, TILE, HD), jnp.bfloat16),
+            pltpu.VMEM((PLANES * tiles, TILE, HD), jnp.bfloat16),
+            pltpu.VMEM((PLANES * tiles, TILE, HD), jnp.bfloat16),
+            pltpu.SemaphoreType.DMA((3,)),
+        ],
+        compiler_params=pltpu.CompilerParams(vmem_limit_bytes=40 * 1024 * 1024),
+        cost_estimate=pl.CostEstimate(
+            flops=work * 8, bytes_accessed=2 * PLANES * tiles * TILE * HD * 2, transcendentals=0
+        ),
+    )(count, lists, ends, *queries, *keys, *values)
+
+
+def relay_plan(queries, keys, values, tile_lists):
+    z = lax.axis_index("z")
+    lanes = SIDE * lax.axis_size("head")
+    width = lanes * HD
+    chunks = queries.shape[1] // width
+    plane_tiles = tile_lists.shape[0] // PLANES
+    at_end = (z == 0) | (z == PLANES - 1)
+
+    def spread(arrays, chunk):
+        cut = [a[:, chunk * width : (chunk + 1) * width] for a in arrays]
+        if len(cut) == 1:
+            got = lax.all_to_all(cut[0], ("y", "head"), split_axis=1, concat_axis=0, tiled=True)
+            return [got.reshape(plane_tiles, TILE, HD)]
+        both = jnp.stack(cut)
+        got = lax.all_to_all(both, ("y", "head"), split_axis=2, concat_axis=1, tiled=True)
+        return [got[i].reshape(plane_tiles, TILE, HD) for i in range(len(cut))]
+
+    def send(array, pairs):
+        return lax.ppermute(array, "z", pairs)
+
+    far = z >= PLANES // 2
+    rows = jnp.stack(
+        [
+            lax.dynamic_slice_in_dim(tile_lists, z * plane_tiles, plane_tiles, 0),
+            lax.dynamic_slice_in_dim(tile_lists, (z ^ 1) * plane_tiles, plane_tiles, 0),
+        ]
+    ).reshape(2 * plane_tiles, -1)
+    plane = rows // plane_tiles
+    plane = jnp.where(far, PLANES - 1 - plane, plane)
+    near = jnp.where(far, PLANES - 1 - z, z)
+    slot = jnp.where(plane < 2, plane ^ near, plane)
+    lists = slot * plane_tiles + rows % plane_tiles
+    ends = at_end.astype(jnp.int32).reshape(1)
+    inner_count = jnp.where(at_end, 0, 2 * plane_tiles).astype(jnp.int32).reshape(1)
+    own_count = jnp.full((1,), plane_tiles, jnp.int32)
+
+    done = []
+    for chunk in range(chunks):
+        last = chunk == chunks - 1
+        if chunk == 0:
+            (own_k,) = spread([keys], chunk)
+            own_v, own_q = spread([values, queries], chunk)
+        else:
+            own_k, own_v, own_q = spread([keys, values, queries], chunk)
+        held = []
+        for own in (own_k, own_v):
+            beside = send(own, SWAP if last else INWARD)
+            across = send(own, CROSS)
+            beyond = send(beside, CROSS)
+            got = [own, beside, across, beyond]
+            if last:
+                got += [send(across, OUTWARD), send(beyond, OUTWARD)]
+            held.append(got)
+        if last:
+            mixed = attend(own_count, lists[:plane_tiles], ends, [own_q], held[0], held[1])
+        else:
+            near_q = send(own_q, INWARD)
+            both = attend(inner_count, lists, ends, [own_q, near_q], held[0], held[1])
+            back = send(both[plane_tiles:], OUTWARD)
+            mixed = jnp.where(at_end, back, both[:plane_tiles])
+        mixed = mixed.reshape(plane_tiles * TILE, HD)
+        done.append(lax.all_to_all(mixed, ("y", "head"), split_axis=0, concat_axis=1, tiled=True))
+    return jnp.concatenate(done, axis=1)
+
+
 def solution(mesh):
-    placed = (
-        P(("groups", "seq", "head"), None),
-        P(("groups", "seq", "head"), None),
-        P(("groups", "seq", "head"), None),
-        P("groups", None),
-    )
+    seq_count, head_count = mesh.shape["seq"], mesh.shape["head"]
+    if seq_count == PLANES * SIDE:
+        planned = Mesh(mesh.devices.reshape(-1, PLANES, SIDE, head_count), AXES)
+        plan, tokens = relay_plan, AXES
+    else:
+        planned, plan, tokens = mesh, slot_plan, ("groups", "seq", "head")
+    placed = P(tokens, None)
     return jax.shard_map(
-        per_device,
-        mesh=mesh,
-        in_specs=placed,
-        out_specs=P(("groups", "seq", "head"), None),
+        plan,
+        mesh=planned,
+        in_specs=(placed, placed, placed, P("groups", None)),
+        out_specs=placed,
         check_vma=False,
     )

time: 593 us -> 314 us (0.53)
  waiting for transfers between devices: 265 us -> 106 us
  local copies, waits for them, and re-layouts: 172 us -> 34.6 us
  matrix products: 78.2 us -> 0 us
  Pallas kernels: 0 us -> 78 us
  starting transfers between devices: 19.3 us -> 82.4 us
  other arithmetic: 44.7 us -> 6.02 us
  blocking collectives: 6.15 us -> 0 us
    all_to_all x4 -> x7, waiting for transfers between devices: 265 us -> 49.4 us  [the longest x3 29.9 us: spread(): lax.all_to_all(both, ('y', 'head'), split_axis=2, concat_axis=1, tiled=True)]
    gather x32 -> x0, local copies, waits for them, and re-layouts: 121 us -> none  [the longest x16 60.5 us: score_tile(): gathered = key_flat[row_index]]
    dot_general x33 -> x0, matrix products: 78.2 us -> none  [the longest x16 40.6 us: mix_tile(): jnp.einsum('hqkt,khtd->qhd', rounded, gathered, preferred_element_type=jn...]
    pallas_call x0 -> x3, Pallas kernels: none -> 78 us  [attend(): pl.pallas_call(kernel, out_shape=jax.ShapeDtypeStruct((rows, TILE, HD), j...]
    ppermute x0 -> x26, waiting for transfers between devices: none -> 56.3 us  [send(): return lax.ppermute(array, 'z', pairs)]
    ppermute x0 -> x26, starting transfers between devices: none -> 55.4 us  [send(): return lax.ppermute(array, 'z', pairs)]
    reduce_sum x17 -> x0, other arithmetic: 41.1 us -> none  [the longest x16 40.7 us: score_tile(): row_total = jnp.sum(weights, axis=(2, 3))]
    dynamic_update_slice x16 -> x0, local copies, waits for them, and re-layouts: 10.5 us -> none  [per_device(): attended = lax.map(joined_tile, (query_tiles, slot_index))]
  transfers between devices with their start and end apart: 4 -> 33, of which waited for: 2 -> 15; matrix products, arithmetic and copies ran while one was open for 6% -> 11% of each run, Pallas kernels for 0% -> 25%
where the time goes in v1:
time: 314 us; the launch traced here: 307 us
  waiting for transfers between devices  106 us (34%)
  starting transfers between devices  82.4 us (26%)
  Pallas kernels  78 us (25%)
  local copies, waits for them, and re-layouts  34.6 us (11%)
  other arithmetic  6.02 us (2%)
    pallas_call x3, Pallas kernels, attend(): pl.pallas_call(kernel, out_shape=jax.ShapeDtypeStruct((rows, TILE, HD), j...  78 us
    ppermute x26, waiting for transfers between devices, send(): return lax.ppermute(array, 'z', pairs)  56.3 us
    ppermute x26, starting transfers between devices, send(): return lax.ppermute(array, 'z', pairs)  55.4 us
    all_to_all x3, waiting for transfers between devices, spread(): lax.all_to_all(both, ('y', 'head'), split_axis=2, concat_axis=1, tiled=True)  29.9 us
    all_to_all x3, waiting for transfers between devices, relay_plan(): lax.all_to_all(mixed, ('y', 'head'), split_axis=0, concat_axis=1, tiled=T...  15.6 us
    all_to_all x3, starting transfers between devices, spread(): lax.all_to_all(both, ('y', 'head'), split_axis=2, concat_axis=1, tiled=True)  12.4 us
    all_to_all x3, starting transfers between devices, relay_plan(): lax.all_to_all(mixed, ('y', 'head'), split_axis=0, concat_axis=1, tiled=T...  11.1 us
    another operation x4, local copies, waits for them, and re-layouts, spread(): both = jnp.stack(cut)  10.9 us
  transfers between devices with their start and end apart: 33, of which 15 were waited for; matrix products, arithmetic and copies ran while one was open for 11% of the time, Pallas kernels for 25%

profile of v1, /device:TPU:18, one launch (start us, length us, event | category | flops | bytes accessed | tf_op | source)
XLA Modules:
  0.0 307.3 jit_solution(16304691942353788680)
XLA Ops:
  3.4 3.5 %all-to-all-start.1 = ((bf16[512,4,128]{2,0,1:T(8,128)(2,1)}), bf16[512,4,128]{2,0,1:T(8,128)(2,1)S(1)}, u32[]{:S(2)}, u32[]{:S(2)}) async-start(bf16[512,4,128]{2,0,1:T(8,128)(2,1)} %bitcast.84), calls=%async_computation.1 | async-start | bytes 1048576 | tf_op jit(solution)/shard_map/all_to_all | solution.py:219
  6.9 2.7 slice_bitcast_fusion.7
  11.8 3.9 %all-to-all-done.1 = bf16[512,4,128]{2,0,1:T(8,128)(2,1)S(1)} async-done(((bf16[512,4,128]{2,0,1:T(8,128)(2,1)}), bf16[512,4,128]{2,0,1:T(8,128)(2,1)S(1)}, u32[]{:S(2)}, u32[]{:S(2)}) %all-to-all-start.1) | async-done | bytes 524320 | tf_op jit(solution)/shard_map/all_to_all | solution.py:219
  15.7 3.5 %all-to-all-start = ((bf16[2,512,512]{1,0,2:T(2,128)(2,1)}), bf16[2,512,512]{1,0,2:T(2,128)(2,1)S(1)}, u32[]{:S(2)}, u32[]{:S(2)}) async-start(bf16[2,512,512]{1,0,2:T(2,128)(2,1)} %copy.37), calls=%async_computation | async-start | bytes 2097152 | tf_op jit(solution)/shard_map/all_to_all | solution.py:222
  20.8 3.0 copy.41
  23.8 9.9 %all-to-all-done = bf16[2,512,512]{1,0,2:T(2,128)(2,1)S(1)} async-done(((bf16[2,512,512]{1,0,2:T(2,128)(2,1)}), bf16[2,512,512]{1,0,2:T(2,128)(2,1)S(1)}, u32[]{:S(2)}, u32[]{:S(2)}) %all-to-all-start) | async-done | bytes 1048608 | tf_op jit(solution)/shard_map/all_to_all | solution.py:222
  34.6 4.5 %all-to-all-start.3 = ((bf16[3,512,512]{1,0,2:T(4,128)(2,1)}), bf16[3,512,512]{1,0,2:T(4,128)(2,1)}, u32[]{:S(2)}, u32[]{:S(2)}) async-start(bf16[3,512,512]{1,0,2:T(4,128)(2,1)} %copy.41), calls=%async_computation.3 | async-start | bytes 4194304 | tf_op jit(solution)/shard_map/all_to_all | solution.py:222
  41.8 3.0 copy.44
  44.8 20.0 %all-to-all-done.3 = bf16[3,512,512]{1,0,2:T(4,128)(2,1)} async-done(((bf16[3,512,512]{1,0,2:T(4,128)(2,1)}), bf16[3,512,512]{1,0,2:T(4,128)(2,1)}, u32[]{:S(2)}, u32[]{:S(2)}) %all-to-all-start.3) | async-done | bytes 1572896 | tf_op jit(solution)/shard_map/all_to_all | solution.py:222
  64.8 4.4 %all-to-all-start.5 = ((bf16[3,512,512]{1,0,2:T(4,128)(2,1)}), bf16[3,512,512]{1,0,2:T(4,128)(2,1)}, u32[]{:S(2)}, u32[]{:S(2)}) async-start(bf16[3,512,512]{1,0,2:T(4,128)(2,1)} %copy.44), calls=%async_computation.5 | async-start | bytes 4194304 | tf_op jit(solution)/shard_map/all_to_all | solution.py:222
  76.3 3.5 %collective-permute-start.5 = (bf16[32,64,128]{2,1,0:T(8,128)(2,1)S(1)}, bf16[32,64,128]{2,1,0:T(8,128)(2,1)S(1)}, u32[]{:S(2)}, u32[]{:S(2)}) collective-permute-start(bf16[32,64,128]{2,1,0:T(8,128)(2,1)S(1)} %bitcast.96), channel_id=1, source_target_pairs={{4,8},{8,4},{5,9},{9,5},{6,10},{10,6},{7,11},{11,7},{20,24},{24,20... | collective-permute-start | bytes 1572872 | tf_op jit(solution)/shard_map/ppermute | solution.py:226
  83.5 4.3 %copy.42 = bf16[3,512,4,128]{3,1,2,0:T(8,128)(2,1)} copy(bf16[3,512,4,128]{1,0,3,2:T(4,128)(2,1)} %bitcast.19) | data formatting | bytes 3145728 | tf_op jit(solution)/shard_map/all_to_all | solution.py:222
  91.7 3.5 %collective-permute-start.10 = (bf16[32,64,128]{2,1,0:T(8,128)(2,1)}, bf16[32,64,128]{2,1,0:T(8,128)(2,1)}, u32[]{:S(2)}, u32[]{:S(2)}) collective-permute-start(bf16[32,64,128]{2,1,0:T(8,128)(2,1)} %bitcast.22.refs_3_), channel_id=1, source_target_pairs={{4,8},{8,4},{5,9},{9,5},{6,10},{10,6},{7,11},{11,7},{20,24},{24,20... | collective-permute-start | bytes 1572872 | tf_op jit(solution)/shard_map/ppermute | solution.py:226
  98.4 4.5 %collective-permute-done.refs_2_ = bf16[32,64,128]{2,1,0:T(8,128)(2,1)} collective-permute-done((bf16[32,64,128]{2,1,0:T(8,128)(2,1)S(1)}, bf16[32,64,128]{2,1,0:T(8,128)(2,1)}, u32[]{:S(2)}, u32[]{:S(2)}) %collective-permute-start) | collective-permute-done | bytes 524320 | tf_op jit(solution)/shard_map/ppermute | solution.py:226
  103.0 3.5 %collective-permute-start.13 = (bf16[32,64,128]{2,1,0:T(8,128)(2,1)}, bf16[32,64,128]{2,1,0:T(8,128)(2,1)}, u32[]{:S(2)}, u32[]{:S(2)}) collective-permute-start(bf16[32,64,128]{2,1,0:T(8,128)(2,1)} %bitcast.23.refs_7_), channel_id=1, source_target_pairs={{4,8},{8,4},{5,9},{9,5},{6,10},{10,6},{7,11},{11,7},{20,24},{24,20... | collective-permute-start | bytes 1572872 | tf_op jit(solution)/shard_map/ppermute | solution.py:226
  111.0 4.3 %copy.45 = bf16[3,512,4,128]{3,1,2,0:T(8,128)(2,1)} copy(bf16[3,512,4,128]{1,0,3,2:T(4,128)(2,1)} %bitcast.29) | data formatting | bytes 3145728 | tf_op jit(solution)/shard_map/all_to_all | solution.py:222
  118.2 7.2 %collective-permute-done.12.refs_8_ = bf16[32,64,128]{2,1,0:T(8,128)(2,1)} collective-permute-done((bf16[32,64,128]{2,1,0:T(8,128)(2,1)}, bf16[32,64,128]{2,1,0:T(8,128)(2,1)}, u32[]{:S(2)}, u32[]{:S(2)}) %collective-permute-start.12) | collective-permute-done | bytes 524320 | tf_op jit(solution)/shard_map/ppermute | solution.py:226
  127.5 3.5 %collective-permute-done.13.refs_9_ = bf16[32,64,128]{2,1,0:T(8,128)(2,1)} collective-permute-done((bf16[32,64,128]{2,1,0:T(8,128)(2,1)}, bf16[32,64,128]{2,1,0:T(8,128)(2,1)}, u32[]{:S(2)}, u32[]{:S(2)}) %collective-permute-start.13) | collective-permute-done | bytes 524320 | tf_op jit(solution)/shard_map/ppermute | solution.py:226
  133.3 8.9 %collective-permute-done.6.refs_10_ = bf16[32,64,128]{2,1,0:T(8,128)(2,1)} collective-permute-done((bf16[32,64,128]{2,1,0:T(8,128)(2,1)}, bf16[32,64,128]{2,1,0:T(8,128)(2,1)}, u32[]{:S(2)}, u32[]{:S(2)}) %collective-permute-start.6) | collective-permute-done | bytes 524320 | tf_op jit(solution)/shard_map/ppermute | solution.py:226
  144.6 30.3 %shard_map.46 = bf16[64,64,128]{2,1,0:T(8,128)(2,1)S(1)} custom-call(s32[1]{0:T(128)} %bitcast.count, s32[64,24]{1,0:T(8,128)S(1)} %fusion.lists, s32[1]{0:T(128)} %bitcast.4.refs_0_, bf16[32,64,128]{2,1,0:T(8,128)(2,1)S(1)} %bitcast.99, bf16[32,64,128]{2,1,0:T(8,128)(2,1)} %collective-permute-done.refs_2_, bf16[32,64,128]{2,1,0:T(8,128)(2,1)S(1)} %bitcast.87, ...), custom_call_target="tpu_custom_call" | custom-call | flops 25769803776 | bytes 4194304 | tf_op jit(solution)/shard_map/pallas_call | solution.py:189
  175.0 3.5 %collective-permute-start.17 = (bf16[32,64,128]{2,1,0:T(8,128)(2,1)S(1)}, bf16[32,64,128]{2,1,0:T(8,128)(2,1)}, u32[]{:S(2)}, u32[]{:S(2)}) collective-permute-start(bf16[32,64,128]{2,1,0:T(8,128)(2,1)S(1)} %bitcast.92), channel_id=1, source_target_pairs={{4,8},{8,4},{5,9},{9,5},{6,10},{10,6},{7,11},{11,7},{20,24},{24,20... | collective-permute-start | bytes 1572872 | tf_op jit(solution)/shard_map/ppermute | solution.py:226
  180.9 3.5 %collective-permute-start.18 = (bf16[32,64,128]{2,1,0:T(8,128)(2,1)S(1)}, bf16[32,64,128]{2,1,0:T(8,128)(2,1)}, u32[]{:S(2)}, u32[]{:S(2)}) collective-permute-start(bf16[32,64,128]{2,1,0:T(8,128)(2,1)S(1)} %collective-permute-done.16.refs_3_), channel_id=1, source_target_pairs={{4,8},{8,4},{5,9},{9,5},{6,10},{10,6},{7,11},{11,7},{20,24},{24,20... | collective-permute-start | bytes 1572872 | tf_op jit(solution)/shard_map/ppermute | solution.py:226
  188.1 30.6 %shard_map.47 = bf16[64,64,128]{2,1,0:T(8,128)(2,1)S(1)} custom-call(s32[1]{0:T(128)} %bitcast.count, s32[64,24]{1,0:T(8,128)S(1)} %fusion.lists, s32[1]{0:T(128)} %bitcast.4.refs_0_, bf16[32,64,128]{2,1,0:T(8,128)(2,1)S(1)} %bitcast.101, bf16[32,64,128]{2,1,0:T(8,128)(2,1)S(1)} %collective-permute-done.8.refs_2_, bf16[32,64,128]{2,1,0:T(8,128)(2,1)} %bitcast.22.refs_3_, ...), custom_call_target="tpu_custom_call" | custom-call | flops 25769803776 | bytes 4194304 | tf_op jit(solution)/shard_map/pallas_call | solution.py:189
  230.9 4.1 %all-to-all-start.2 = ((bf16[4,512,128]{2,1,0:T(8,128)(2,1)}), bf16[4,512,128]{2,1,0:T(8,128)(2,1)}, u32[]{:S(2)}, u32[]{:S(2)}) async-start(bf16[4,512,128]{2,1,0:T(8,128)(2,1)} %bitcast.14), calls=%async_computation.2 | async-start | bytes 1048576 | tf_op jit(solution)/shard_map/all_to_all | solution.py:269
  236.0 8.0 %all-to-all-done.2 = bf16[4,512,128]{2,1,0:T(8,128)(2,1)} async-done(((bf16[4,512,128]{2,1,0:T(8,128)(2,1)}), bf16[4,512,128]{2,1,0:T(8,128)(2,1)}, u32[]{:S(2)}, u32[]{:S(2)}) %all-to-all-start.2) | async-done | bytes 524320 | tf_op jit(solution)/shard_map/all_to_all | solution.py:269
  244.0 3.5 %all-to-all-start.4 = ((bf16[4,512,128]{2,1,0:T(8,128)(2,1)}), bf16[4,512,128]{2,1,0:T(8,128)(2,1)S(1)}, u32[]{:S(2)}, u32[]{:S(2)}) async-start(bf16[4,512,128]{2,1,0:T(8,128)(2,1)} %bitcast.106), calls=%async_computation.4 | async-start | bytes 1048576 | tf_op jit(solution)/shard_map/all_to_all | solution.py:269
  247.4 8.6 %collective-permute-done.24.refs_12_ = bf16[32,64,128]{2,1,0:T(8,128)(2,1)} collective-permute-done((bf16[32,64,128]{2,1,0:T(8,128)(2,1)}, bf16[32,64,128]{2,1,0:T(8,128)(2,1)}, u32[]{:S(2)}, u32[]{:S(2)}) %collective-permute-start.24) | collective-permute-done | bytes 524320 | tf_op jit(solution)/shard_map/ppermute | solution.py:226
  256.0 11.2 %collective-permute-done.20.refs_7_ = bf16[32,64,128]{2,1,0:T(8,128)(2,1)} collective-permute-done((bf16[32,64,128]{2,1,0:T(8,128)(2,1)}, bf16[32,64,128]{2,1,0:T(8,128)(2,1)}, u32[]{:S(2)}, u32[]{:S(2)}) %collective-permute-start.20) | collective-permute-done | bytes 524320 | tf_op jit(solution)/shard_map/ppermute | solution.py:226
  267.3 8.3 %collective-permute-done.25.refs_13_ = bf16[32,64,128]{2,1,0:T(8,128)(2,1)} collective-permute-done((bf16[32,64,128]{2,1,0:T(8,128)(2,1)}, bf16[32,64,128]{2,1,0:T(8,128)(2,1)}, u32[]{:S(2)}, u32[]{:S(2)}) %collective-permute-start.25) | collective-permute-done | bytes 524320 | tf_op jit(solution)/shard_map/ppermute | solution.py:226
  276.6 17.1 %shard_map.48 = bf16[32,64,128]{2,1,0:T(8,128)(2,1)} custom-call(s32[1]{0:T(128)} %constant.47.clone.1.count, s32[32,24]{1,0:T(8,128)S(1)} %slice.105.lists, s32[1]{0:T(128)} %bitcast.4.refs_0_, bf16[32,64,128]{2,1,0:T(8,128)(2,1)S(1)} %bitcast.94, bf16[32,64,128]{2,1,0:T(8,128)(2,1)S(1)} %bitcast.93, bf16[32,64,128]{2,1,0:T(8,128)(2,1)S(1)} %copy-done.8, ...), custom_call_target="tpu_custom_call" | custom-call | flops 12884901888 | bytes 4194304 | tf_op jit(solution)/shard_map/pallas_call | solution.py:189
  293.7 3.5 %all-to-all-start.6 = ((bf16[4,512,128]{2,1,0:T(8,128)(2,1)}), bf16[4,512,128]{2,1,0:T(8,128)(2,1)S(1)}, u32[]{:S(2)}, u32[]{:S(2)}) async-start(bf16[4,512,128]{2,1,0:T(8,128)(2,1)} %bitcast.34), calls=%async_computation.6 | async-start | bytes 1048576 | tf_op jit(solution)/shard_map/all_to_all | solution.py:269
  298.4 7.6 %all-to-all-done.6 = bf16[4,512,128]{2,1,0:T(8,128)(2,1)S(1)} async-done(((bf16[4,512,128]{2,1,0:T(8,128)(2,1)}), bf16[4,512,128]{2,1,0:T(8,128)(2,1)S(1)}, u32[]{:S(2)}, u32[]{:S(2)}) %all-to-all-start.6) | async-done | bytes 524320 | tf_op jit(solution)/shard_map/all_to_all | solution.py:269
  (97 shorter events, 65.4 us)
Async XLA Ops:
  15.7 18.0 %all-to-all-start = ((bf16[2,512,512]{1,0,2:T(2,128)(2,1)}), bf16[2,512,512]{1,0,2:T(2,128)(2,1)S(1)}, u32[]{:S(2)}, u32[]{:S(2)}) async-start(bf16[2,512,512]{1,0,2:T(2,128)(2,1)} %copy.37), calls=%async_computation | async-start | bytes 2097152 | tf_op jit(solution)/shard_map/all_to_all | solution.py:222
  34.6 30.2 %all-to-all-start.3 = ((bf16[3,512,512]{1,0,2:T(4,128)(2,1)}), bf16[3,512,512]{1,0,2:T(4,128)(2,1)}, u32[]{:S(2)}, u32[]{:S(2)}) async-start(bf16[3,512,512]{1,0,2:T(4,128)(2,1)} %copy.41), calls=%async_computation.3 | async-start | bytes 4194304 | tf_op jit(solution)/shard_map/all_to_all | solution.py:222
  39.1 42.0 %collective-permute-start.1 = (bf16[32,64,128]{2,1,0:T(8,128)(2,1)S(1)}, bf16[32,64,128]{2,1,0:T(8,128)(2,1)S(1)}, u32[]{:S(2)}, u32[]{:S(2)}) collective-permute-start(bf16[32,64,128]{2,1,0:T(8,128)(2,1)S(1)} %bitcast.85), channel_id=1, source_target_pairs={{0,4},{12,8},{1,5},{13,9},{2,6},{14,10},{3,7},{15,11},{16,20},{28,... | collective-permute-start | bytes 1572872 | tf_op jit(solution)/shard_map/ppermute | solution.py:226
  64.8 46.2 %all-to-all-start.5 = ((bf16[3,512,512]{1,0,2:T(4,128)(2,1)}), bf16[3,512,512]{1,0,2:T(4,128)(2,1)}, u32[]{:S(2)}, u32[]{:S(2)}) async-start(bf16[3,512,512]{1,0,2:T(4,128)(2,1)} %copy.44), calls=%async_computation.5 | async-start | bytes 4194304 | tf_op jit(solution)/shard_map/all_to_all | solution.py:222
  69.3 21.1 %collective-permute-start.2 = (bf16[32,64,128]{2,1,0:T(8,128)(2,1)S(1)}, bf16[32,64,128]{2,1,0:T(8,128)(2,1)S(1)}, u32[]{:S(2)}, u32[]{:S(2)}) collective-permute-start(bf16[32,64,128]{2,1,0:T(8,128)(2,1)S(1)} %bitcast.86), channel_id=1, source_target_pairs={{4,8},{8,4},{5,9},{9,5},{6,10},{10,6},{7,11},{11,7},{20,24},{24,20... | collective-permute-start | bytes 1572872 | tf_op jit(solution)/shard_map/ppermute | solution.py:226
  75.0 16.8 %collective-permute-start.4 = (bf16[32,64,128]{2,1,0:T(8,128)(2,1)S(1)}, bf16[32,64,128]{2,1,0:T(8,128)(2,1)}, u32[]{:S(2)}, u32[]{:S(2)}) collective-permute-start(bf16[32,64,128]{2,1,0:T(8,128)(2,1)S(1)} %bitcast.95), channel_id=1, source_target_pairs={{0,4},{12,8},{1,5},{13,9},{2,6},{14,10},{3,7},{15,11},{16,20},{28,... | collective-permute-start | bytes 1572872 | tf_op jit(solution)/shard_map/ppermute | solution.py:226
  76.3 20.9 %collective-permute-start.5 = (bf16[32,64,128]{2,1,0:T(8,128)(2,1)S(1)}, bf16[32,64,128]{2,1,0:T(8,128)(2,1)S(1)}, u32[]{:S(2)}, u32[]{:S(2)}) collective-permute-start(bf16[32,64,128]{2,1,0:T(8,128)(2,1)S(1)} %bitcast.96), channel_id=1, source_target_pairs={{4,8},{8,4},{5,9},{9,5},{6,10},{10,6},{7,11},{11,7},{20,24},{24,20... | collective-permute-start | bytes 1572872 | tf_op jit(solution)/shard_map/ppermute | solution.py:226
  79.8 23.2 %collective-permute-start = (bf16[32,64,128]{2,1,0:T(8,128)(2,1)S(1)}, bf16[32,64,128]{2,1,0:T(8,128)(2,1)}, u32[]{:S(2)}, u32[]{:S(2)}) collective-permute-start(bf16[32,64,128]{2,1,0:T(8,128)(2,1)S(1)} %bitcast.98), channel_id=1, source_target_pairs={{0,4},{12,8},{1,5},{13,9},{2,6},{14,10},{3,7},{15,11},{16,20},{28,... | collective-permute-start | bytes 1572872 | tf_op jit(solution)/shard_map/ppermute | solution.py:226
  81.1 27.4 %collective-permute-start.3 = (bf16[32,64,128]{2,1,0:T(8,128)(2,1)S(1)}, bf16[32,64,128]{2,1,0:T(8,128)(2,1)}, u32[]{:S(2)}, u32[]{:S(2)}) collective-permute-start(bf16[32,64,128]{2,1,0:T(8,128)(2,1)S(1)} %collective-permute-done.1.refs_4_), channel_id=1, source_target_pairs={{4,8},{8,4},{5,9},{9,5},{6,10},{10,6},{7,11},{11,7},{20,24},{24,20... | collective-permute-start | bytes 1572872 | tf_op jit(solution)/shard_map/ppermute | solution.py:226
  90.4 26.5 %collective-permute-start.9 = (bf16[32,64,128]{2,1,0:T(8,128)(2,1)}, bf16[32,64,128]{2,1,0:T(8,128)(2,1)}, u32[]{:S(2)}, u32[]{:S(2)}) collective-permute-start(bf16[32,64,128]{2,1,0:T(8,128)(2,1)} %bitcast.22.refs_3_), channel_id=1, source_target_pairs={{0,4},{12,8},{1,5},{13,9},{2,6},{14,10},{3,7},{15,11},{16,20},{28,... | collective-permute-start | bytes 1572872 | tf_op jit(solution)/shard_map/ppermute | solution.py:226
  91.7 33.7 %collective-permute-start.10 = (bf16[32,64,128]{2,1,0:T(8,128)(2,1)}, bf16[32,64,128]{2,1,0:T(8,128)(2,1)}, u32[]{:S(2)}, u32[]{:S(2)}) collective-permute-start(bf16[32,64,128]{2,1,0:T(8,128)(2,1)} %bitcast.22.refs_3_), channel_id=1, source_target_pairs={{4,8},{8,4},{5,9},{9,5},{6,10},{10,6},{7,11},{11,7},{20,24},{24,20... | collective-permute-start | bytes 1572872 | tf_op jit(solution)/shard_map/ppermute | solution.py:226
  97.2 28.3 %collective-permute-start.12 = (bf16[32,64,128]{2,1,0:T(8,128)(2,1)}, bf16[32,64,128]{2,1,0:T(8,128)(2,1)}, u32[]{:S(2)}, u32[]{:S(2)}) collective-permute-start(bf16[32,64,128]{2,1,0:T(8,128)(2,1)} %bitcast.23.refs_7_), channel_id=1, source_target_pairs={{0,4},{12,8},{1,5},{13,9},{2,6},{14,10},{3,7},{15,11},{16,20},{28,... | collective-permute-start | bytes 1572872 | tf_op jit(solution)/shard_map/ppermute | solution.py:226
  103.0 28.0 %collective-permute-start.13 = (bf16[32,64,128]{2,1,0:T(8,128)(2,1)}, bf16[32,64,128]{2,1,0:T(8,128)(2,1)}, u32[]{:S(2)}, u32[]{:S(2)}) collective-permute-start(bf16[32,64,128]{2,1,0:T(8,128)(2,1)} %bitcast.23.refs_7_), channel_id=1, source_target_pairs={{4,8},{8,4},{5,9},{9,5},{6,10},{10,6},{7,11},{11,7},{20,24},{24,20... | collective-permute-start | bytes 1572872 | tf_op jit(solution)/shard_map/ppermute | solution.py:226
  108.5 33.7 %collective-permute-start.6 = (bf16[32,64,128]{2,1,0:T(8,128)(2,1)}, bf16[32,64,128]{2,1,0:T(8,128)(2,1)}, u32[]{:S(2)}, u32[]{:S(2)}) collective-permute-start(bf16[32,64,128]{2,1,0:T(8,128)(2,1)} %collective-permute-done.4.refs_8_), channel_id=1, source_target_pairs={{4,8},{8,4},{5,9},{9,5},{6,10},{10,6},{7,11},{11,7},{20,24},{24,20... | collective-permute-start | bytes 1572872 | tf_op jit(solution)/shard_map/ppermute | solution.py:226
  116.9 58.0 %collective-permute-start.8 = (bf16[32,64,128]{2,1,0:T(8,128)(2,1)S(1)}, bf16[32,64,128]{2,1,0:T(8,128)(2,1)S(1)}, u32[]{:S(2)}, u32[]{:S(2)}) collective-permute-start(bf16[32,64,128]{2,1,0:T(8,128)(2,1)S(1)} %bitcast.100), channel_id=1, source_target_pairs={{0,4},{12,8},{1,5},{13,9},{2,6},{14,10},{3,7},{15,11},{16,20},{28,... | collective-permute-start | bytes 1572872 | tf_op jit(solution)/shard_map/ppermute | solution.py:226
  125.4 53.0 %collective-permute-start.16 = (bf16[32,64,128]{2,1,0:T(8,128)(2,1)S(1)}, bf16[32,64,128]{2,1,0:T(8,128)(2,1)S(1)}, u32[]{:S(2)}, u32[]{:S(2)}) collective-permute-start(bf16[32,64,128]{2,1,0:T(8,128)(2,1)S(1)} %bitcast.91), channel_id=1, source_target_pairs={{0,4},{4,0},{8,12},{12,8},{1,5},{5,1},{9,13},{13,9},{2,6},{6,2},{1... | collective-permute-start | bytes 1572872 | tf_op jit(solution)/shard_map/ppermute | solution.py:226
  125.5 55.4 %collective-permute-start.21 = (bf16[32,64,128]{2,1,0:T(8,128)(2,1)S(1)}, bf16[32,64,128]{2,1,0:T(8,128)(2,1)S(1)}, u32[]{:S(2)}, u32[]{:S(2)}) collective-permute-start(bf16[32,64,128]{2,1,0:T(8,128)(2,1)S(1)} %bitcast.88), channel_id=1, source_target_pairs={{0,4},{4,0},{8,12},{12,8},{1,5},{5,1},{9,13},{13,9},{2,6},{6,2},{1... | collective-permute-start | bytes 1572872 | tf_op jit(solution)/shard_map/ppermute | solution.py:226
  131.0 53.4 %collective-permute-start.11 = (bf16[32,64,128]{2,1,0:T(8,128)(2,1)}, bf16[32,64,128]{2,1,0:T(8,128)(2,1)S(1)}, u32[]{:S(2)}, u32[]{:S(2)}) collective-permute-start(bf16[32,64,128]{2,1,0:T(8,128)(2,1)} %collective-permute-done.9.refs_4_), channel_id=1, source_target_pairs={{4,8},{8,4},{5,9},{9,5},{6,10},{10,6},{7,11},{11,7},{20,24},{24,20... | collective-permute-start | bytes 1572872 | tf_op jit(solution)/shard_map/ppermute | solution.py:226
  142.2 44.5 %collective-permute-start.14 = (bf16[32,64,128]{2,1,0:T(8,128)(2,1)}, bf16[32,64,128]{2,1,0:T(8,128)(2,1)S(1)}, u32[]{:S(2)}, u32[]{:S(2)}) collective-permute-start(bf16[32,64,128]{2,1,0:T(8,128)(2,1)} %collective-permute-done.12.refs_8_), channel_id=1, source_target_pairs={{4,8},{8,4},{5,9},{9,5},{6,10},{10,6},{7,11},{11,7},{20,24},{24,20... | collective-permute-start | bytes 1572872 | tf_op jit(solution)/shard_map/ppermute | solution.py:226
  175.0 44.6 %collective-permute-start.17 = (bf16[32,64,128]{2,1,0:T(8,128)(2,1)S(1)}, bf16[32,64,128]{2,1,0:T(8,128)(2,1)}, u32[]{:S(2)}, u32[]{:S(2)}) collective-permute-start(bf16[32,64,128]{2,1,0:T(8,128)(2,1)S(1)} %bitcast.92), channel_id=1, source_target_pairs={{4,8},{8,4},{5,9},{9,5},{6,10},{10,6},{7,11},{11,7},{20,24},{24,20... | collective-permute-start | bytes 1572872 | tf_op jit(solution)/shard_map/ppermute | solution.py:226
  178.5 43.2 %collective-permute-start.22 = (bf16[32,64,128]{2,1,0:T(8,128)(2,1)S(1)}, bf16[32,64,128]{2,1,0:T(8,128)(2,1)}, u32[]{:S(2)}, u32[]{:S(2)}) collective-permute-start(bf16[32,64,128]{2,1,0:T(8,128)(2,1)S(1)} %bitcast.89), channel_id=1, source_target_pairs={{4,8},{8,4},{5,9},{9,5},{6,10},{10,6},{7,11},{11,7},{20,24},{24,20... | collective-permute-start | bytes 1572872 | tf_op jit(solution)/shard_map/ppermute | solution.py:226
  180.9 42.9 %collective-permute-start.18 = (bf16[32,64,128]{2,1,0:T(8,128)(2,1)S(1)}, bf16[32,64,128]{2,1,0:T(8,128)(2,1)}, u32[]{:S(2)}, u32[]{:S(2)}) collective-permute-start(bf16[32,64,128]{2,1,0:T(8,128)(2,1)S(1)} %collective-permute-done.16.refs_3_), channel_id=1, source_target_pairs={{4,8},{8,4},{5,9},{9,5},{6,10},{10,6},{7,11},{11,7},{20,24},{24,20... | collective-permute-start | bytes 1572872 | tf_op jit(solution)/shard_map/ppermute | solution.py:226
  184.4 41.5 %collective-permute-start.23 = (bf16[32,64,128]{2,1,0:T(8,128)(2,1)S(1)}, bf16[32,64,128]{2,1,0:T(8,128)(2,1)}, u32[]{:S(2)}, u32[]{:S(2)}) collective-permute-start(bf16[32,64,128]{2,1,0:T(8,128)(2,1)S(1)} %collective-permute-done.21.refs_9_), channel_id=1, source_target_pairs={{4,8},{8,4},{5,9},{9,5},{6,10},{10,6},{7,11},{11,7},{20,24},{24,20... | collective-permute-start | bytes 1572872 | tf_op jit(solution)/shard_map/ppermute | solution.py:226
  186.7 41.2 %collective-permute-start.7 = (bf16[32,64,128]{2,1,0:T(8,128)(2,1)S(1)}, bf16[32,64,128]{2,1,0:T(8,128)(2,1)S(1)}, u32[]{:S(2)}, u32[]{:S(2)}) collective-permute-start(bf16[32,64,128]{2,1,0:T(8,128)(2,1)S(1)} %slice.98), channel_id=1, source_target_pairs={{4,0},{8,12},{5,1},{9,13},{6,2},{10,14},{7,3},{11,15},{20,16},{24,... | collective-permute-start | bytes 1572872 | tf_op jit(solution)/shard_map/ppermute | solution.py:226
  219.6 15.5 %collective-permute-start.15 = (bf16[32,64,128]{2,1,0:T(8,128)(2,1)}, bf16[32,64,128]{2,1,0:T(8,128)(2,1)}, u32[]{:S(2)}, u32[]{:S(2)}) collective-permute-start(bf16[32,64,128]{2,1,0:T(8,128)(2,1)} %slice.103), channel_id=1, source_target_pairs={{4,0},{8,12},{5,1},{9,13},{6,2},{10,14},{7,3},{11,15},{20,16},{24,... | collective-permute-start | bytes 1572872 | tf_op jit(solution)/shard_map/ppermute | solution.py:226
  221.7 25.7 %collective-permute-start.19 = (bf16[32,64,128]{2,1,0:T(8,128)(2,1)}, bf16[32,64,128]{2,1,0:T(8,128)(2,1)}, u32[]{:S(2)}, u32[]{:S(2)}) collective-permute-start(bf16[32,64,128]{2,1,0:T(8,128)(2,1)} %collective-permute-done.17.refs_4_), channel_id=1, source_target_pairs={{4,0},{8,12},{5,1},{9,13},{6,2},{10,14},{7,3},{11,15},{20,16},{24,... | collective-permute-start | bytes 1572872 | tf_op jit(solution)/shard_map/ppermute | solution.py:226
  223.8 32.3 %collective-permute-start.24 = (bf16[32,64,128]{2,1,0:T(8,128)(2,1)}, bf16[32,64,128]{2,1,0:T(8,128)(2,1)}, u32[]{:S(2)}, u32[]{:S(2)}) collective-permute-start(bf16[32,64,128]{2,1,0:T(8,128)(2,1)} %collective-permute-done.22.refs_10_), channel_id=1, source_target_pairs={{4,0},{8,12},{5,1},{9,13},{6,2},{10,14},{7,3},{11,15},{20,16},{24,... | collective-permute-start | bytes 1572872 | tf_op jit(solution)/shard_map/ppermute | solution.py:226
  225.9 41.4 %collective-permute-start.20 = (bf16[32,64,128]{2,1,0:T(8,128)(2,1)}, bf16[32,64,128]{2,1,0:T(8,128)(2,1)}, u32[]{:S(2)}, u32[]{:S(2)}) collective-permute-start(bf16[32,64,128]{2,1,0:T(8,128)(2,1)} %collective-permute-done.18.refs_5_), channel_id=1, source_target_pairs={{4,0},{8,12},{5,1},{9,13},{6,2},{10,14},{7,3},{11,15},{20,16},{24,... | collective-permute-start | bytes 1572872 | tf_op jit(solution)/shard_map/ppermute | solution.py:226
  228.0 47.6 %collective-permute-start.25 = (bf16[32,64,128]{2,1,0:T(8,128)(2,1)}, bf16[32,64,128]{2,1,0:T(8,128)(2,1)}, u32[]{:S(2)}, u32[]{:S(2)}) collective-permute-start(bf16[32,64,128]{2,1,0:T(8,128)(2,1)} %collective-permute-done.23.refs_11_), channel_id=1, source_target_pairs={{4,0},{8,12},{5,1},{9,13},{6,2},{10,14},{7,3},{11,15},{20,16},{24,... | collective-permute-start | bytes 1572872 | tf_op jit(solution)/shard_map/ppermute | solution.py:226
  230.9 13.0 %all-to-all-start.2 = ((bf16[4,512,128]{2,1,0:T(8,128)(2,1)}), bf16[4,512,128]{2,1,0:T(8,128)(2,1)}, u32[]{:S(2)}, u32[]{:S(2)}) async-start(bf16[4,512,128]{2,1,0:T(8,128)(2,1)} %bitcast.14), calls=%async_computation.2 | async-start | bytes 1048576 | tf_op jit(solution)/shard_map/all_to_all | solution.py:269
  244.0 49.7 %all-to-all-start.4 = ((bf16[4,512,128]{2,1,0:T(8,128)(2,1)}), bf16[4,512,128]{2,1,0:T(8,128)(2,1)S(1)}, u32[]{:S(2)}, u32[]{:S(2)}) async-start(bf16[4,512,128]{2,1,0:T(8,128)(2,1)} %bitcast.106), calls=%async_computation.4 | async-start | bytes 1048576 | tf_op jit(solution)/shard_map/all_to_all | solution.py:269
  293.7 12.3 %all-to-all-start.6 = ((bf16[4,512,128]{2,1,0:T(8,128)(2,1)}), bf16[4,512,128]{2,1,0:T(8,128)(2,1)S(1)}, u32[]{:S(2)}, u32[]{:S(2)}) async-start(bf16[4,512,128]{2,1,0:T(8,128)(2,1)} %bitcast.34), calls=%async_computation.6 | async-start | bytes 1048576 | tf_op jit(solution)/shard_map/all_to_all | solution.py:269
  (17 other events, 329.8 us)

commit v2 on v0

--- a/solution.py
+++ b/solution.py
@@ -1,7 +1,12 @@
+import functools
+import math
+
 import jax
 import jax.numpy as jnp
 from jax import lax
-from jax.sharding import PartitionSpec as P
+from jax.experimental import pallas as pl
+from jax.experimental.pallas import tpu as pltpu
+from jax.sharding import Mesh, PartitionSpec as P
 
 HD = 128
 TILE = 64
@@ -36,7 +41,7 @@
     return outgoing.reshape(seq_count, capacity, count, local_heads, tile_rows, head_dim)
 
 
-def per_device(queries, keys, values, tile_lists):
+def slot_plan(queries, keys, values, tile_lists):
     seq_count = lax.axis_size("seq")
     head_count = lax.axis_size("head")
     head_dim = HD
@@ -102,17 +107,288 @@
     return lax.all_to_all(attended, "head", split_axis=0, concat_axis=1, tiled=True)
 
 
+PLANES = 4
+SIDE = 2
+AXES = ("groups", "z", "y", "head")
+RANKS = ("y", "head")
+INWARD = [(0, 1), (3, 2)]
+OUTWARD = [(1, 0), (2, 3)]
+CROSS = [(1, 2), (2, 1)]
+EXPONENT = HD**-0.5 * math.log2(math.e)
+UNROLL = 4
+COST = 11 * 10**9
+VMEM_LIMIT = 60 * 1024 * 1024
+
+
+def shuffle_kernel(*refs, parts, source_count):
+    sources, outs = refs[:source_count], refs[source_count : source_count + len(parts)]
+    bufs, sems = refs[source_count + len(parts) : -1], refs[-1]
+    loads, stores = {}, []
+    for wanted in parts:
+        for which, chunk in wanted:
+            width = outs[0].shape[0] * HD
+            columns = pl.ds(chunk * width, width)
+            loads[which, chunk] = pltpu.make_async_copy(
+                sources[which].at[:, columns], bufs[which].at[:, columns], sems.at[len(loads)]
+            )
+            loads[which, chunk].start()
+    for out, wanted in zip(outs, parts):
+        for at, (which, chunk) in enumerate(wanted):
+            loads[which, chunk].wait()
+            for lane in range(out.shape[0]):
+                column = (chunk * out.shape[0] + lane) * HD
+                store = pltpu.make_async_copy(
+                    bufs[which].at[:, pl.ds(column, HD)],
+                    out.at[lane, at],
+                    sems.at[len(loads) + len(stores)],
+                )
+                store.start()
+                stores.append(store)
+    for store in stores:
+        store.wait()
+
+
+def shuffle(arrays, lanes, parts, name):
+    rows = arrays[0].shape[0]
+    kernel = functools.partial(shuffle_kernel, parts=parts, source_count=len(arrays))
+    moved = sum(len(p) for p in parts)
+    return pl.pallas_call(
+        kernel,
+        out_shape=[
+            jax.ShapeDtypeStruct((lanes, len(p), rows, HD), arrays[0].dtype) for p in parts
+        ],
+        in_specs=[pl.BlockSpec(memory_space=pl.ANY)] * len(arrays),
+        out_specs=[pl.BlockSpec(memory_space=pl.ANY)] * len(parts),
+        scratch_shapes=[pltpu.VMEM(a.shape, a.dtype) for a in arrays]
+        + [pltpu.SemaphoreType.DMA((moved * (lanes + 1),))],
+        compiler_params=pltpu.CompilerParams(vmem_limit_bytes=VMEM_LIMIT),
+        cost_estimate=pl.CostEstimate(
+            flops=0, bytes_accessed=2 * moved * lanes * rows * HD * 2, transcendentals=0
+        ),
+        name=name,
+    )(*arrays)
+
+
+def gather_kernel(*refs):
+    sources, out, buf, sems = refs[:-3], refs[-3], refs[-2], refs[-1]
+    loads = []
+    for source in sources:
+        for at in range(source.shape[1]):
+            for lane in range(source.shape[0]):
+                column = pl.ds(len(loads) * HD, HD)
+                load = pltpu.make_async_copy(
+                    source.at[lane, at], buf.at[:, column], sems.at[len(loads)]
+                )
+                load.start()
+                loads.append(load)
+    for load in loads:
+        load.wait()
+    store = pltpu.make_async_copy(buf, out, sems.at[len(loads)])
+    store.start()
+    store.wait()
+
+
+def gather_out(parts):
+    rows = parts[0].shape[2]
+    blocks = sum(p.shape[0] * p.shape[1] for p in parts)
+    return pl.pallas_call(
+        gather_kernel,
+        out_shape=jax.ShapeDtypeStruct((rows, blocks * HD), parts[0].dtype),
+        in_specs=[pl.BlockSpec(memory_space=pl.ANY)] * len(parts),
+        out_specs=pl.BlockSpec(memory_space=pl.ANY),
+        scratch_shapes=[
+            pltpu.VMEM((rows, blocks * HD), parts[0].dtype),
+            pltpu.SemaphoreType.DMA((blocks + 1,)),
+        ],
+        compiler_params=pltpu.CompilerParams(vmem_limit_bytes=VMEM_LIMIT),
+        name="gather_out",
+    )(*parts)
+
+
+def attend_kernel(count, lists, query, *refs, chunk, ats):
+    picks = refs[: 2 * PLANES]
+    out, query_buf, key_buf, value_buf, score_buf, sems = refs[2 * PLANES :]
+    lanes, _, shard_tiles = query.shape[:3]
+    tiles = lanes * shard_tiles
+    top_count = lists.shape[1]
+    blank = jnp.zeros((TILE, HD), jnp.bfloat16)
+
+    def beside(left, right):
+        return jnp.concatenate([left, right], axis=1)
+
+    @pl.when(count[0] > 0)
+    def _():
+        for lane in range(lanes):
+            place = pl.ds(lane * shard_tiles, shard_tiles)
+            pltpu.make_async_copy(query.at[lane, chunk], query_buf.at[place], sems.at[0]).start()
+        for kind, buf in enumerate((key_buf, value_buf)):
+            for slot in range(PLANES):
+                source, at = picks[kind * PLANES + slot], ats[kind]
+                for lane in range(lanes):
+                    place = pl.ds((slot * lanes + lane) * shard_tiles, shard_tiles)
+                    pltpu.make_async_copy(
+                        source.at[lane, at], buf.at[place], sems.at[1 + kind]
+                    ).start()
+        pltpu.make_async_copy(query_buf, query_buf, sems.at[0]).wait()
+        pltpu.make_async_copy(key_buf, key_buf, sems.at[1]).wait()
+
+        def listed(buf, pair, t):
+            return beside(buf[lists[2 * pair, t]], buf[lists[2 * pair + 1, t]])
+
+        def score(pair, at):
+            wide = jnp.concatenate(
+                [beside(query_buf[2 * pair], blank), beside(blank, query_buf[2 * pair + 1])], axis=0
+            )
+            keys = jnp.concatenate([listed(key_buf, pair, t) for t in range(top_count)], axis=0)
+            score_buf[at] = lax.dot_general(
+                wide, keys, (((1,), (1,)), ((), ())), preferred_element_type=jnp.float32
+            )
+
+        def mix(pair, at):
+            scores = score_buf[at]
+            row_top = jnp.max(scores, axis=1, keepdims=True)
+            weights = jnp.exp2((scores - row_top) * EXPONENT)
+            row_total = jnp.sum(weights, axis=1, keepdims=True)
+            values = jnp.concatenate([listed(value_buf, pair, t) for t in range(top_count)], axis=0)
+            mixture = jnp.dot(
+                weights.astype(jnp.bfloat16), values, preferred_element_type=jnp.float32
+            )
+            first = mixture[:TILE, :HD] / row_total[:TILE]
+            second = mixture[TILE:, HD:] / row_total[TILE:]
+            out[2 * pair] = first.astype(jnp.bfloat16)
+            out[2 * pair + 1] = second.astype(jnp.bfloat16)
+
+        score(0, 0)
+        pltpu.make_async_copy(value_buf, value_buf, sems.at[2]).wait()
+
+        def step(at, carry):
+            for sub in range(UNROLL):
+                pair = at * UNROLL + sub
+                score(jnp.minimum(pair + 1, tiles // 2 - 1), (sub + 1) % 2)
+                mix(pair, sub % 2)
+            return carry
+
+        lax.fori_loop(0, tiles // 2 // UNROLL, step, 0)
+
+
+def attend(count, lists, query, keys, values, ats, chunk, name):
+    tiles, top_count = lists.shape
+    lanes = query.shape[0]
+    shaped = (lanes, -1, tiles // lanes, TILE, HD)
+    return pl.pallas_call(
+        functools.partial(attend_kernel, chunk=chunk, ats=ats),
+        out_shape=jax.ShapeDtypeStruct((tiles, TILE, HD), jnp.bfloat16),
+        in_specs=[pl.BlockSpec(memory_space=pltpu.SMEM)] * 2
+        + [pl.BlockSpec(memory_space=pl.ANY)] * (1 + 2 * PLANES),
+        out_specs=pl.BlockSpec(memory_space=pltpu.VMEM),
+        scratch_shapes=[
+            pltpu.VMEM((tiles, TILE, HD), jnp.bfloat16),
+            pltpu.VMEM((PLANES * tiles, TILE, HD), jnp.bfloat16),
+            pltpu.VMEM((PLANES * tiles, TILE, HD), jnp.bfloat16),
+            pltpu.VMEM((2, 2 * TILE, top_count * TILE), jnp.float32),
+            pltpu.SemaphoreType.DMA((3,)),
+        ],
+        compiler_params=pltpu.CompilerParams(vmem_limit_bytes=VMEM_LIMIT),
+        cost_estimate=pl.CostEstimate(flops=COST, bytes_accessed=1, transcendentals=0),
+        name=name,
+    )(count, lists, query.reshape(shaped), *[a.reshape(shaped) for a in (*keys, *values)])
+
+
+def after(array, *others):
+    return lax.optimization_barrier((array, *others))[0]
+
+
+def relay_plan(queries, keys, values, tile_lists):
+    z = lax.axis_index("z")
+    lanes = SIDE * lax.axis_size("head")
+    chunks = queries.shape[1] // (lanes * HD)
+    plane_tiles = tile_lists.shape[0] // PLANES
+    at_end = (z == 0) | (z == PLANES - 1)
+
+    def swap(array):
+        return lax.all_to_all(array, RANKS, split_axis=0, concat_axis=0, tiled=True)
+
+    def send(array, pairs, name):
+        with jax.named_scope(name):
+            return lax.ppermute(array, "z", pairs)
+
+    far = z >= PLANES // 2
+    rows = jnp.stack(
+        [
+            lax.dynamic_slice_in_dim(tile_lists, z * plane_tiles, plane_tiles, 0),
+            lax.dynamic_slice_in_dim(tile_lists, (z ^ 1) * plane_tiles, plane_tiles, 0),
+        ]
+    )
+    plane = rows // plane_tiles
+    plane = jnp.where(far, PLANES - 1 - plane, plane)
+    near = jnp.where(far, PLANES - 1 - z, z)
+    slot = jnp.where(plane < 2, plane ^ near, plane)
+    lists = slot * plane_tiles + rows % plane_tiles
+    count = jnp.where(at_end, 0, 1).astype(jnp.int32).reshape(1)
+
+    (first,) = shuffle([keys, values], lanes, [[(0, 0), (1, 0)]], "shuffle_first")
+    own_0 = swap(first)
+    rest = shuffle(
+        [queries, keys, values],
+        lanes,
+        [[(0, c) for c in range(chunks)]] + [[(1, c), (2, c)] for c in range(1, chunks)],
+        "shuffle_rest",
+    )
+    in_0 = send(own_0, INWARD, "in_0")
+    cross_0 = send(own_0, CROSS, "cross_0")
+    own_1 = swap(after(rest[1], own_0))
+    relay_0 = send(in_0, CROSS, "relay_0")
+    in_1 = send(after(own_1, in_0), INWARD, "in_1")
+    cross_1 = send(after(own_1, cross_0), CROSS, "cross_1")
+    asked = swap(after(rest[0], own_1, cross_0, in_0))
+    own_2 = swap(after(rest[2], asked, in_1))
+    in_q = send(after(asked, in_1), INWARD, "in_q")
+    in_2 = send(after(own_2, in_1), INWARD, "in_2")
+    cross_2 = send(after(own_2, relay_0), CROSS, "cross_2")
+    relay_1 = send(after(in_1, relay_0), CROSS, "relay_1")
+
+    done = []
+
+    def one(at, chunk, query, pairs):
+        return attend(count, lists[at], query, pairs, pairs, (0, 1), chunk, f"attend_{chunk}{at}")
+
+    def home(beside, chunk):
+        return send(beside, OUTWARD, f"out_{chunk}")
+
+    def finish(parts):
+        mixed = []
+        for own, home in parts:
+            mixed.append(jnp.where(at_end, home, own).reshape(lanes, -1, HD))
+        return mixed[0][:, None] if len(mixed) == 1 else jnp.stack(mixed, axis=1)
+
+    pairs = [own_0, in_0, cross_0, relay_0]
+    mine_0 = one(0, 0, after(asked, cross_1, own_2), pairs)
+    theirs_0 = one(1, 0, after(in_q, mine_0), pairs)
+    relay_2 = send(after(in_2, cross_1, relay_1), CROSS, "relay_2")
+    pairs = [own_1, in_1, cross_1, relay_1]
+    mine_1 = one(0, 1, after(asked, theirs_0, in_2), pairs)
+    theirs_1 = one(1, 1, after(in_q, mine_1), pairs)
+    home_0, home_1 = home(theirs_0, 0), home(theirs_1, 1)
+    pairs = [own_2, in_2, cross_2, relay_2]
+    theirs_2 = one(1, 2, after(in_q, theirs_1), pairs)
+    mine_2 = one(0, 2, after(asked, theirs_2), pairs)
+    early = swap(finish([(mine_0, after(home_0, theirs_2)), (mine_1, after(home_1, theirs_2))]))
+    late = swap(after(finish([(mine_2, home(theirs_2, 2))]), early))
+    return gather_out([early, late])
+
+
 def solution(mesh):
-    placed = (
-        P(("groups", "seq", "head"), None),
-        P(("groups", "seq", "head"), None),
-        P(("groups", "seq", "head"), None),
-        P("groups", None),
-    )
+    seq_count, head_count = mesh.shape["seq"], mesh.shape["head"]
+    if seq_count == PLANES * SIDE:
+        planned = Mesh(mesh.devices.reshape(-1, PLANES, SIDE, head_count), AXES)
+        plan, tokens = relay_plan, AXES
+    else:
+        planned, plan, tokens = mesh, slot_plan, ("groups", "seq", "head")
+    placed = P(tokens, None)
     return jax.shard_map(
-        per_device,
-        mesh=mesh,
-        in_specs=placed,
-        out_specs=P(("groups", "seq", "head"), None),
+        plan,
+        mesh=planned,
+        in_specs=(placed, placed, placed, P("groups", None)),
+        out_specs=placed,
         check_vma=False,
     )

time: 593 us -> 221 us (0.37)
  waiting for transfers between devices: 265 us -> 56.8 us
  local copies, waits for them, and re-layouts: 172 us -> 2.85 us
  matrix products: 78.2 us -> 0 us
  Pallas kernels: 0 us -> 72.9 us
  blocking collectives: 6.15 us -> 48.7 us
  other arithmetic: 44.7 us -> 2.35 us
  starting transfers between devices: 19.3 us -> 35.1 us
    all_to_all x4 -> x3, waiting for transfers between devices: 265 us -> 2.51 us  [swap(): return lax.all_to_all(array, RANKS, split_axis=0, concat_axis=0, tiled=True)]
    gather x32 -> x0, local copies, waits for them, and re-layouts: 121 us -> none  [the longest x16 60.5 us: score_tile(): gathered = key_flat[row_index]]
    dot_general x33 -> x0, matrix products: 78.2 us -> none  [the longest x16 40.6 us: mix_tile(): jnp.einsum('hqkt,khtd->qhd', rounded, gathered, preferred_element_type=jn...]
    pallas_call x0 -> x9, Pallas kernels: none -> 72.9 us  [the longest x6 64.8 us: attend(): pl.pallas_call(functools.partial(attend_kernel, chunk=chunk, ats=ats), ou...]
    ppermute x0 -> x13, waiting for transfers between devices: none -> 54.3 us  [send(): return lax.ppermute(array, 'z', pairs)]
    all_to_all x1 -> x3, blocking collectives: 6.15 us -> 48.7 us  [swap(): return lax.all_to_all(array, RANKS, split_axis=0, concat_axis=0, tiled=True)]
    reduce_sum x17 -> x0, other arithmetic: 41.1 us -> none  [the longest x16 40.7 us: score_tile(): row_total = jnp.sum(weights, axis=(2, 3))]
    ppermute x0 -> x13, starting transfers between devices: none -> 24.5 us  [send(): return lax.ppermute(array, 'z', pairs)]
  transfers between devices with their start and end apart: 4 -> 16, of which waited for: 2 -> 8; matrix products, arithmetic and copies ran while one was open for 6% -> 1% of each run, Pallas kernels for 0% -> 31%
where the time goes in v2:
time: 221 us; the launch traced here: 219 us
  Pallas kernels  72.9 us (33%)
  waiting for transfers between devices  56.8 us (26%)
  blocking collectives  48.7 us (22%)
  starting transfers between devices  35.1 us (16%)
  local copies, waits for them, and re-layouts  2.85 us (1%)
  other arithmetic  2.35 us (1%)
    pallas_call x6, Pallas kernels, attend(): pl.pallas_call(functools.partial(attend_kernel, chunk=chunk, ats=ats), ou...  64.8 us
    ppermute x13, waiting for transfers between devices, send(): return lax.ppermute(array, 'z', pairs)  54.3 us
    all_to_all x3, blocking collectives, swap(): return lax.all_to_all(array, RANKS, split_axis=0, concat_axis=0, tiled=True)  48.7 us
    ppermute x13, starting transfers between devices, send(): return lax.ppermute(array, 'z', pairs)  24.5 us
    all_to_all x3, starting transfers between devices, swap(): return lax.all_to_all(array, RANKS, split_axis=0, concat_axis=0, tiled=True)  10.6 us
    pallas_call x2, Pallas kernels, shuffle(): pl.pallas_call(kernel, out_shape=[jax.ShapeDtypeStruct((lanes, len(p), ro...  5.38 us
  transfers between devices with their start and end apart: 16, of which 8 were waited for; matrix products, arithmetic and copies ran while one was open for 1% of the time, Pallas kernels for 31%

profile of v2, /device:TPU:18, one launch (start us, length us, event | category | flops | bytes accessed | tf_op | source)
XLA Modules:
  0.0 219.0 jit_solution(14166837922156928652)
XLA Ops:
  0.0 2.1 shuffle_first.1
  2.1 18.0 %all_to_all.30 = bf16[4,2,512,128]{3,2,1,0:T(8,128)(2,1)S(1)} all-to-all(bf16[4,2,512,128]{3,2,1,0:T(8,128)(2,1)} %shuffle_first.1), channel_id=1, replica_groups=mesh['groups'=2,'z'=4,'y'=2,'head'=2] {'y','head'}, dimensions={0} | all-to-all | bytes 2097152 | tf_op jit(solution)/shard_map/all_to_all | solution.py:309
  21.3 2.4 %collective-permute-start = (bf16[4,2,512,128]{3,2,1,0:T(8,128)(2,1)S(1)}, bf16[4,2,512,128]{3,2,1,0:T(8,128)(2,1)S(1)}, u32[]{:S(2)}, u32[]{:S(2)}) collective-permute-start(bf16[4,2,512,128]{3,2,1,0:T(8,128)(2,1)S(1)} %all_to_all.30), channel_id=1, source_target_pairs={{4,8},{8,4},{5,9},{9,5},{6,10},{10,6},{7,11},{11,7},{20,24},{24,20... | collective-permute-start | bytes 3145736 | tf_op jit(solution)/shard_map/cross_0/ppermute | solution.py:313
  23.7 3.3 %shuffle_rest.1 = (bf16[4,3,512,128]{3,2,1,0:T(8,128)(2,1)}, bf16[4,2,512,128]{3,2,1,0:T(8,128)(2,1)}, bf16[4,2,512,128]{3,2,1,0:T(8,128)(2,1)}) custom-call(bf16[512,1536]{1,0:T(8,128)(2,1)} %refs_0_.2, bf16[512,1536]{1,0:T(8,128)(2,1)} %refs_0_.3, bf16[512,1536]{1,0:T(8,128)(2,1)} %refs_1_.3), custom_call_target="tpu_custom_call" | custom-call | bytes 7340032 | tf_op jit(solution)/shard_map/shuffle_rest/pallas_call | solution.py:155
  27.0 18.8 %all_to_all.31 = bf16[4,2,512,128]{3,2,1,0:T(8,128)(2,1)} all-to-all(bf16[4,2,512,128]{3,2,1,0:T(8,128)(2,1)} %get-tuple-element.29), channel_id=1, replica_groups=mesh['groups'=2,'z'=4,'y'=2,'head'=2] {'y','head'}, dimensions={0} | all-to-all | bytes 2097152 | tf_op jit(solution)/shard_map/all_to_all | solution.py:309
  46.5 1.3 collective-permute-done
  48.7 3.6 %all-to-all-start.2 = ((bf16[4,3,512,128]{3,2,1,0:T(8,128)(2,1)}), bf16[4,3,512,128]{3,2,1,0:T(8,128)(2,1)S(1)}, u32[]{:S(2)}, u32[]{:S(2)}) async-start(bf16[4,3,512,128]{3,2,1,0:T(8,128)(2,1)} %get-tuple-element.30), calls=%async_computation.2 | async-start | bytes 3145728 | tf_op jit(solution)/shard_map/all_to_all | solution.py:309
  52.3 1.3 collective-permute-start.2
  53.6 2.4 %collective-permute-start.5 = (bf16[4,2,512,128]{3,2,1,0:T(8,128)(2,1)}, bf16[4,2,512,128]{3,2,1,0:T(8,128)(2,1)}, u32[]{:S(2)}, u32[]{:S(2)}) collective-permute-start(bf16[4,2,512,128]{3,2,1,0:T(8,128)(2,1)} %copy-done.7), channel_id=1, source_target_pairs={{4,8},{8,4},{5,9},{9,5},{6,10},{10,6},{7,11},{11,7},{20,24},{24,20... | collective-permute-start | bytes 3145736 | tf_op jit(solution)/shard_map/relay_0/ppermute | solution.py:313
  56.0 3.5 %collective-permute-start.4 = (bf16[4,2,512,128]{3,2,1,0:T(8,128)(2,1)}, bf16[4,2,512,128]{3,2,1,0:T(8,128)(2,1)}, u32[]{:S(2)}, u32[]{:S(2)}) collective-permute-start(bf16[4,2,512,128]{3,2,1,0:T(8,128)(2,1)} %all_to_all.31), channel_id=1, source_target_pairs={{4,8},{8,4},{5,9},{9,5},{6,10},{10,6},{7,11},{11,7},{20,24},{24,20... | collective-permute-start | bytes 3145736 | tf_op jit(solution)/shard_map/cross_1/ppermute | solution.py:313
  59.5 20.7 %collective-permute-done.2 = bf16[4,2,512,128]{3,2,1,0:T(8,128)(2,1)} collective-permute-done((bf16[4,2,512,128]{3,2,1,0:T(8,128)(2,1)}, bf16[4,2,512,128]{3,2,1,0:T(8,128)(2,1)}, u32[]{:S(2)}, u32[]{:S(2)}) %collective-permute-start.2) | collective-permute-done | bytes 1048608 | tf_op jit(solution)/shard_map/in_1/ppermute | solution.py:313
  80.2 3.5 %all-to-all-start.3 = ((bf16[4,2,512,128]{3,2,1,0:T(8,128)(2,1)}), bf16[4,2,512,128]{3,2,1,0:T(8,128)(2,1)S(1)}, u32[]{:S(2)}, u32[]{:S(2)}) async-start(bf16[4,2,512,128]{3,2,1,0:T(8,128)(2,1)} %get-tuple-element.35), calls=%async_computation.3 | async-start | bytes 2097152 | tf_op jit(solution)/shard_map/all_to_all | solution.py:309
  85.9 2.3 %collective-permute-start.8 = (bf16[4,2,512,128]{3,2,1,0:T(8,128)(2,1)}, bf16[4,2,512,128]{3,2,1,0:T(8,128)(2,1)}, u32[]{:S(2)}, u32[]{:S(2)}) collective-permute-start(bf16[4,2,512,128]{3,2,1,0:T(8,128)(2,1)} %collective-permute-done.2), channel_id=1, source_target_pairs={{4,8},{8,4},{5,9},{9,5},{6,10},{10,6},{7,11},{11,7},{20,24},{24,20... | collective-permute-start | bytes 3145736 | tf_op jit(solution)/shard_map/relay_1/ppermute | solution.py:313
  88.3 16.0 %collective-permute-done.4 = bf16[4,2,512,128]{3,2,1,0:T(8,128)(2,1)} collective-permute-done((bf16[4,2,512,128]{3,2,1,0:T(8,128)(2,1)}, bf16[4,2,512,128]{3,2,1,0:T(8,128)(2,1)}, u32[]{:S(2)}, u32[]{:S(2)}) %collective-permute-start.4) | collective-permute-done | bytes 1048608 | tf_op jit(solution)/shard_map/cross_1/ppermute | solution.py:313
  105.5 2.4 %collective-permute-start.9 = (bf16[4,2,512,128]{3,2,1,0:T(8,128)(2,1)S(1)}, bf16[4,2,512,128]{3,2,1,0:T(8,128)(2,1)}, u32[]{:S(2)}, u32[]{:S(2)}) collective-permute-start(bf16[4,2,512,128]{3,2,1,0:T(8,128)(2,1)S(1)} %all-to-all-done.3), channel_id=1, source_target_pairs={{4,8},{8,4},{5,9},{9,5},{6,10},{10,6},{7,11},{11,7},{20,24},{24,20... | collective-permute-start | bytes 3145736 | tf_op jit(solution)/shard_map/cross_2/ppermute | solution.py:313
  107.9 10.8 %attend_00.1 = bf16[32,64,128]{2,1,0:T(8,128)(2,1)} custom-call(s32[1]{0:T(128)} %bitcast.count, s32[32,24]{1,0:T(8,128)} %get-tuple-element.49.lists, bf16[4,3,8,64,128]{4,3,2,1,0:T(8,128)(2,1)} %bitcast.31, bf16[4,2,8,64,128]{4,3,2,1,0:T(8,128)(2,1)} %bitcast.38, bf16[4,2,8,64,128]{4,3,2,1,0:T(8,128)(2,1)} %bitcast.44, ...), custom_call_target="tpu_custom_call" | custom-call | flops 11000000512 | bytes 1 | tf_op jit(solution)/shard_map/attend_00/pallas_call | solution.py:278
  118.7 4.2 %collective-permute-done.3 = bf16[4,3,512,128]{3,2,1,0:T(8,128)(2,1)} collective-permute-done((bf16[4,3,512,128]{3,2,1,0:T(8,128)(2,1)S(1)}, bf16[4,3,512,128]{3,2,1,0:T(8,128)(2,1)}, u32[]{:S(2)}, u32[]{:S(2)}) %collective-permute-start.3) | collective-permute-done | bytes 1572896 | tf_op jit(solution)/shard_map/in_q/ppermute | solution.py:313
  122.9 10.8 %attend_01.1 = bf16[32,64,128]{2,1,0:T(8,128)(2,1)} custom-call(s32[1]{0:T(128)} %bitcast.count, s32[32,24]{1,0:T(8,128)} %get-tuple-element.50.lists, bf16[4,3,8,64,128]{4,3,2,1,0:T(8,128)(2,1)} %bitcast.10.query, bf16[4,2,8,64,128]{4,3,2,1,0:T(8,128)(2,1)} %bitcast.40, bf16[4,2,8,64,128]{4,3,2,1,0:T(8,128)(2,1)} %bitcast.46, ...), custom_call_target="tpu_custom_call" | custom-call | flops 11000000512 | bytes 1 | tf_op jit(solution)/shard_map/attend_01/pallas_call | solution.py:278
  133.7 1.3 collective-permute-start.6
  135.0 9.9 %collective-permute-done.7 = bf16[4,2,512,128]{3,2,1,0:T(8,128)(2,1)} collective-permute-done((bf16[4,2,512,128]{3,2,1,0:T(8,128)(2,1)S(1)}, bf16[4,2,512,128]{3,2,1,0:T(8,128)(2,1)}, u32[]{:S(2)}, u32[]{:S(2)}) %collective-permute-start.7) | collective-permute-done | bytes 1048608 | tf_op jit(solution)/shard_map/in_2/ppermute | solution.py:313
  144.9 2.3 %collective-permute-start.10 = (bf16[4,2,512,128]{3,2,1,0:T(8,128)(2,1)}, bf16[4,2,512,128]{3,2,1,0:T(8,128)(2,1)S(1)}, u32[]{:S(2)}, u32[]{:S(2)}) collective-permute-start(bf16[4,2,512,128]{3,2,1,0:T(8,128)(2,1)} %collective-permute-done.7), channel_id=1, source_target_pairs={{4,8},{8,4},{5,9},{9,5},{6,10},{10,6},{7,11},{11,7},{20,24},{24,20... | collective-permute-start | bytes 3145736 | tf_op jit(solution)/shard_map/relay_2/ppermute | solution.py:313
  147.3 10.8 %attend_10.1 = bf16[32,64,128]{2,1,0:T(8,128)(2,1)} custom-call(s32[1]{0:T(128)} %bitcast.count, s32[32,24]{1,0:T(8,128)} %get-tuple-element.49.lists, bf16[4,3,8,64,128]{4,3,2,1,0:T(8,128)(2,1)} %bitcast.32, bf16[4,2,8,64,128]{4,3,2,1,0:T(8,128)(2,1)} %bitcast.12.refs_0_.refs_4_, bf16[4,2,8,64,128]{4,3,2,1,0:T(8,128)(2,1)} %bitcast.13.refs_1_.refs_5_, ...), custom_call_target="tpu_custom_call" | custom-call | flops 11000000512 | bytes 1 | tf_op jit(solution)/shard_map/attend_10/pallas_call | solution.py:278
  158.1 10.8 %attend_11.1 = bf16[32,64,128]{2,1,0:T(8,128)(2,1)} custom-call(s32[1]{0:T(128)} %bitcast.count, s32[32,24]{1,0:T(8,128)} %get-tuple-element.50.lists, bf16[4,3,8,64,128]{4,3,2,1,0:T(8,128)(2,1)} %bitcast.16.query, bf16[4,2,8,64,128]{4,3,2,1,0:T(8,128)(2,1)} %bitcast.12.refs_0_.refs_4_, bf16[4,2,8,64,128]{4,3,2,1,0:T(8,128)(2,1)} %bitcast.13.refs_1_.refs_5_, ...), custom_call_target="tpu_custom_call" | custom-call | flops 11000000512 | bytes 1 | tf_op jit(solution)/shard_map/attend_11/pallas_call | solution.py:278
  168.9 1.3 collective-permute-start.11
  170.2 1.6 collective-permute-done.10
  172.8 10.9 %attend_21.1 = bf16[32,64,128]{2,1,0:T(8,128)(2,1)} custom-call(s32[1]{0:T(128)} %bitcast.count, s32[32,24]{1,0:T(8,128)} %get-tuple-element.50.lists, bf16[4,3,8,64,128]{4,3,2,1,0:T(8,128)(2,1)} %bitcast.17.query, bf16[4,2,8,64,128]{4,3,2,1,0:T(8,128)(2,1)} %bitcast.34, bf16[4,2,8,64,128]{4,3,2,1,0:T(8,128)(2,1)} %bitcast.19.refs_1_.refs_5_, ...), custom_call_target="tpu_custom_call" | custom-call | flops 11000000512 | bytes 1 | tf_op jit(solution)/shard_map/attend_21/pallas_call | solution.py:278
  183.7 1.5 collective-permute-start.12
  186.4 3.5 %all-to-all-start.4 = ((bf16[4,2,512,128]{3,2,1,0:T(8,128)(2,1)}), bf16[4,2,512,128]{3,2,1,0:T(8,128)(2,1)S(1)}, u32[]{:S(2)}, u32[]{:S(2)}) async-start(bf16[4,2,512,128]{3,2,1,0:T(8,128)(2,1)} %pad_maximum_fusion), calls=%async_computation.4 | async-start | bytes 2097152 | tf_op jit(solution)/shard_map/all_to_all | solution.py:309
  190.0 10.8 %attend_20.1 = bf16[32,64,128]{2,1,0:T(8,128)(2,1)} custom-call(s32[1]{0:T(128)} %bitcast.count, s32[32,24]{1,0:T(8,128)} %get-tuple-element.49.lists, bf16[4,3,8,64,128]{4,3,2,1,0:T(8,128)(2,1)} %bitcast.33, bf16[4,2,8,64,128]{4,3,2,1,0:T(8,128)(2,1)} %bitcast.36, bf16[4,2,8,64,128]{4,3,2,1,0:T(8,128)(2,1)} %bitcast.19.refs_1_.refs_5_, ...), custom_call_target="tpu_custom_call" | custom-call | flops 11000000512 | bytes 1 | tf_op jit(solution)/shard_map/attend_20/pallas_call | solution.py:278
  201.9 2.5 %all-to-all-done.4.refs_0_ = bf16[4,2,512,128]{3,2,1,0:T(8,128)(2,1)S(1)} async-done(((bf16[4,2,512,128]{3,2,1,0:T(8,128)(2,1)}), bf16[4,2,512,128]{3,2,1,0:T(8,128)(2,1)S(1)}, u32[]{:S(2)}, u32[]{:S(2)}) %all-to-all-start.4) | async-done | bytes 1048608 | tf_op jit(solution)/shard_map/all_to_all | solution.py:309
  204.4 11.9 %all_to_all.32.refs_1_ = bf16[4,1,512,128]{3,2,1,0:T(8,128)(2,1)} all-to-all(bf16[4,1,512,128]{3,2,1,0:T(8,128)(2,1)S(1)} %bitcast.28), channel_id=1, replica_groups=mesh['groups'=2,'z'=4,'y'=2,'head'=2] {'y','head'}, dimensions={0} | all-to-all | bytes 1048576 | tf_op jit(solution)/shard_map/all_to_all | solution.py:309
  216.3 2.7 %gather_out.1 = bf16[512,1536]{1,0:T(8,128)(2,1)} custom-call(bf16[4,2,512,128]{3,2,1,0:T(8,128)(2,1)} %copy-done, bf16[4,1,512,128]{3,2,1,0:T(8,128)(2,1)} %all_to_all.32.refs_1_), custom_call_target="tpu_custom_call" | custom-call | tf_op jit(solution)/shard_map/gather_out/pallas_call | solution.py:194
  (41 shorter events, 9.7 us)
Async XLA Ops:
  20.0 7.0 %copy-start.3 = (bf16[4,2,512,128]{3,2,1,0:T(8,128)(2,1)}, bf16[4,2,512,128]{3,2,1,0:T(8,128)(2,1)S(1)}, u32[]{:S(2)}) copy-start(bf16[4,2,512,128]{3,2,1,0:T(8,128)(2,1)S(1)} %all_to_all.30) | copy-start | bytes 3145732
  20.1 26.4 %collective-permute-start.1 = (bf16[4,2,512,128]{3,2,1,0:T(8,128)(2,1)S(1)}, bf16[4,2,512,128]{3,2,1,0:T(8,128)(2,1)S(1)}, u32[]{:S(2)}, u32[]{:S(2)}) collective-permute-start(bf16[4,2,512,128]{3,2,1,0:T(8,128)(2,1)S(1)} %all_to_all.30), channel_id=1, source_target_pairs={{0,4},{12,8},{1,5},{13,9},{2,6},{14,10},{3,7},{15,11},{16,20},{28,... | collective-permute-start | bytes 3145736 | tf_op jit(solution)/shard_map/in_0/ppermute | solution.py:313
  21.3 26.4 %collective-permute-start = (bf16[4,2,512,128]{3,2,1,0:T(8,128)(2,1)S(1)}, bf16[4,2,512,128]{3,2,1,0:T(8,128)(2,1)S(1)}, u32[]{:S(2)}, u32[]{:S(2)}) collective-permute-start(bf16[4,2,512,128]{3,2,1,0:T(8,128)(2,1)S(1)} %all_to_all.30), channel_id=1, source_target_pairs={{4,8},{8,4},{5,9},{9,5},{6,10},{10,6},{7,11},{11,7},{20,24},{24,20... | collective-permute-start | bytes 3145736 | tf_op jit(solution)/shard_map/cross_0/ppermute | solution.py:313
  46.5 1.3 copy-start.7
  47.8 1.0 copy-start.8
  48.7 31.4 %all-to-all-start.2 = ((bf16[4,3,512,128]{3,2,1,0:T(8,128)(2,1)}), bf16[4,3,512,128]{3,2,1,0:T(8,128)(2,1)S(1)}, u32[]{:S(2)}, u32[]{:S(2)}) async-start(bf16[4,3,512,128]{3,2,1,0:T(8,128)(2,1)} %get-tuple-element.30), calls=%async_computation.2 | async-start | bytes 3145728 | tf_op jit(solution)/shard_map/all_to_all | solution.py:309
  52.3 32.7 %copy-start.6 = (s32[128,24]{0,1:T(8,128)S(1)}, s32[128,24]{0,1:T(8,128)}, u32[]{:S(2)}) copy-start(s32[128,24]{0,1:T(8,128)} %param.7) | copy-start | bytes 36868
  52.3 27.9 %collective-permute-start.2 = (bf16[4,2,512,128]{3,2,1,0:T(8,128)(2,1)}, bf16[4,2,512,128]{3,2,1,0:T(8,128)(2,1)}, u32[]{:S(2)}, u32[]{:S(2)}) collective-permute-start(bf16[4,2,512,128]{3,2,1,0:T(8,128)(2,1)} %all_to_all.31), channel_id=1, source_target_pairs={{0,4},{12,8},{1,5},{13,9},{2,6},{14,10},{3,7},{15,11},{16,20},{28,... | collective-permute-start | bytes 3145736 | tf_op jit(solution)/shard_map/in_1/ppermute | solution.py:313
  53.6 32.3 %collective-permute-start.5 = (bf16[4,2,512,128]{3,2,1,0:T(8,128)(2,1)}, bf16[4,2,512,128]{3,2,1,0:T(8,128)(2,1)}, u32[]{:S(2)}, u32[]{:S(2)}) collective-permute-start(bf16[4,2,512,128]{3,2,1,0:T(8,128)(2,1)} %copy-done.7), channel_id=1, source_target_pairs={{4,8},{8,4},{5,9},{9,5},{6,10},{10,6},{7,11},{11,7},{20,24},{24,20... | collective-permute-start | bytes 3145736 | tf_op jit(solution)/shard_map/relay_0/ppermute | solution.py:313
  56.0 48.3 %collective-permute-start.4 = (bf16[4,2,512,128]{3,2,1,0:T(8,128)(2,1)}, bf16[4,2,512,128]{3,2,1,0:T(8,128)(2,1)}, u32[]{:S(2)}, u32[]{:S(2)}) collective-permute-start(bf16[4,2,512,128]{3,2,1,0:T(8,128)(2,1)} %all_to_all.31), channel_id=1, source_target_pairs={{4,8},{8,4},{5,9},{9,5},{6,10},{10,6},{7,11},{11,7},{20,24},{24,20... | collective-permute-start | bytes 3145736 | tf_op jit(solution)/shard_map/cross_1/ppermute | solution.py:313
  80.2 27.7 %copy-start.1 = (bf16[4,3,512,128]{3,2,1,0:T(8,128)(2,1)}, bf16[4,3,512,128]{3,2,1,0:T(8,128)(2,1)S(1)}, u32[]{:S(2)}) copy-start(bf16[4,3,512,128]{3,2,1,0:T(8,128)(2,1)S(1)} %all-to-all-done.2) | copy-start | bytes 4718596
  80.2 24.1 %all-to-all-start.3 = ((bf16[4,2,512,128]{3,2,1,0:T(8,128)(2,1)}), bf16[4,2,512,128]{3,2,1,0:T(8,128)(2,1)S(1)}, u32[]{:S(2)}, u32[]{:S(2)}) async-start(bf16[4,2,512,128]{3,2,1,0:T(8,128)(2,1)} %get-tuple-element.35), calls=%async_computation.3 | async-start | bytes 2097152 | tf_op jit(solution)/shard_map/all_to_all | solution.py:309
  83.7 39.2 %collective-permute-start.3 = (bf16[4,3,512,128]{3,2,1,0:T(8,128)(2,1)S(1)}, bf16[4,3,512,128]{3,2,1,0:T(8,128)(2,1)}, u32[]{:S(2)}, u32[]{:S(2)}) collective-permute-start(bf16[4,3,512,128]{3,2,1,0:T(8,128)(2,1)S(1)} %all-to-all-done.2), channel_id=1, source_target_pairs={{0,4},{12,8},{1,5},{13,9},{2,6},{14,10},{3,7},{15,11},{16,20},{28,... | collective-permute-start | bytes 4718600 | tf_op jit(solution)/shard_map/in_q/ppermute | solution.py:313
  85.9 59.0 %collective-permute-start.8 = (bf16[4,2,512,128]{3,2,1,0:T(8,128)(2,1)}, bf16[4,2,512,128]{3,2,1,0:T(8,128)(2,1)}, u32[]{:S(2)}, u32[]{:S(2)}) collective-permute-start(bf16[4,2,512,128]{3,2,1,0:T(8,128)(2,1)} %collective-permute-done.2), channel_id=1, source_target_pairs={{4,8},{8,4},{5,9},{9,5},{6,10},{10,6},{7,11},{11,7},{20,24},{24,20... | collective-permute-start | bytes 3145736 | tf_op jit(solution)/shard_map/relay_1/ppermute | solution.py:313
  104.3 14.5 %copy-start.2 = (bf16[4,2,512,128]{3,2,1,0:T(8,128)(2,1)}, bf16[4,2,512,128]{3,2,1,0:T(8,128)(2,1)S(1)}, u32[]{:S(2)}) copy-start(bf16[4,2,512,128]{3,2,1,0:T(8,128)(2,1)S(1)} %all-to-all-done.3) | copy-start | bytes 3145732
  104.3 40.7 %collective-permute-start.7 = (bf16[4,2,512,128]{3,2,1,0:T(8,128)(2,1)S(1)}, bf16[4,2,512,128]{3,2,1,0:T(8,128)(2,1)}, u32[]{:S(2)}, u32[]{:S(2)}) collective-permute-start(bf16[4,2,512,128]{3,2,1,0:T(8,128)(2,1)S(1)} %all-to-all-done.3), channel_id=1, source_target_pairs={{0,4},{12,8},{1,5},{13,9},{2,6},{14,10},{3,7},{15,11},{16,20},{28,... | collective-permute-start | bytes 3145736 | tf_op jit(solution)/shard_map/in_2/ppermute | solution.py:313
  105.5 64.7 %collective-permute-start.9 = (bf16[4,2,512,128]{3,2,1,0:T(8,128)(2,1)S(1)}, bf16[4,2,512,128]{3,2,1,0:T(8,128)(2,1)}, u32[]{:S(2)}, u32[]{:S(2)}) collective-permute-start(bf16[4,2,512,128]{3,2,1,0:T(8,128)(2,1)S(1)} %all-to-all-done.3), channel_id=1, source_target_pairs={{4,8},{8,4},{5,9},{9,5},{6,10},{10,6},{7,11},{11,7},{20,24},{24,20... | collective-permute-start | bytes 3145736 | tf_op jit(solution)/shard_map/cross_2/ppermute | solution.py:313
  133.7 51.5 %collective-permute-start.6 = (bf16[32,64,128]{2,1,0:T(8,128)(2,1)}, bf16[32,64,128]{2,1,0:T(8,128)(2,1)S(1)}, u32[]{:S(2)}, u32[]{:S(2)}) collective-permute-start(bf16[32,64,128]{2,1,0:T(8,128)(2,1)} %attend_01.1), channel_id=1, source_target_pairs={{4,0},{8,12},{5,1},{9,13},{6,2},{10,14},{7,3},{11,15},{20,16},{24,... | collective-permute-start | bytes 1572872 | tf_op jit(solution)/shard_map/out_0/ppermute | solution.py:313
  144.9 26.8 %collective-permute-start.10 = (bf16[4,2,512,128]{3,2,1,0:T(8,128)(2,1)}, bf16[4,2,512,128]{3,2,1,0:T(8,128)(2,1)S(1)}, u32[]{:S(2)}, u32[]{:S(2)}) collective-permute-start(bf16[4,2,512,128]{3,2,1,0:T(8,128)(2,1)} %collective-permute-done.7), channel_id=1, source_target_pairs={{4,8},{8,4},{5,9},{9,5},{6,10},{10,6},{7,11},{11,7},{20,24},{24,20... | collective-permute-start | bytes 3145736 | tf_op jit(solution)/shard_map/relay_2/ppermute | solution.py:313
  168.9 16.4 %collective-permute-start.11 = (bf16[32,64,128]{2,1,0:T(8,128)(2,1)}, bf16[32,64,128]{2,1,0:T(8,128)(2,1)S(1)}, u32[]{:S(2)}, u32[]{:S(2)}) collective-permute-start(bf16[32,64,128]{2,1,0:T(8,128)(2,1)} %attend_11.1), channel_id=1, source_target_pairs={{4,0},{8,12},{5,1},{9,13},{6,2},{10,14},{7,3},{11,15},{20,16},{24,... | collective-permute-start | bytes 1572872 | tf_op jit(solution)/shard_map/out_1/ppermute | solution.py:313
  171.8 1.0 copy-start.9
  172.8 12.4 %copy-start.4 = (bf16[32,64,128]{2,1,0:T(8,128)(2,1)S(1)}, bf16[32,64,128]{2,1,0:T(8,128)(2,1)}, u32[]{:S(2)}) copy-start(bf16[32,64,128]{2,1,0:T(8,128)(2,1)} %attend_00.1) | copy-start | bytes 1572868
  183.7 1.6 copy-start.5
  183.7 17.0 %collective-permute-start.12 = (bf16[32,64,128]{2,1,0:T(8,128)(2,1)}, bf16[32,64,128]{2,1,0:T(8,128)(2,1)S(1)}, u32[]{:S(2)}, u32[]{:S(2)}) collective-permute-start(bf16[32,64,128]{2,1,0:T(8,128)(2,1)} %attend_21.1), channel_id=1, source_target_pairs={{4,0},{8,12},{5,1},{9,13},{6,2},{10,14},{7,3},{11,15},{20,16},{24,... | collective-permute-start | bytes 1572872 | tf_op jit(solution)/shard_map/out_2/ppermute | solution.py:313
  186.4 18.0 %all-to-all-start.4 = ((bf16[4,2,512,128]{3,2,1,0:T(8,128)(2,1)}), bf16[4,2,512,128]{3,2,1,0:T(8,128)(2,1)S(1)}, u32[]{:S(2)}, u32[]{:S(2)}) async-start(bf16[4,2,512,128]{3,2,1,0:T(8,128)(2,1)} %pad_maximum_fusion), calls=%async_computation.4 | async-start | bytes 2097152 | tf_op jit(solution)/shard_map/all_to_all | solution.py:309
  204.4 11.9 %copy-start = (bf16[4,2,512,128]{3,2,1,0:T(8,128)(2,1)}, bf16[4,2,512,128]{3,2,1,0:T(8,128)(2,1)S(1)}, u32[]{:S(2)}) copy-start(bf16[4,2,512,128]{3,2,1,0:T(8,128)(2,1)S(1)} %all-to-all-done.4.refs_0_) | copy-start | bytes 3145732
